TPU v7x, 32 devices: a whole 2x2x4 slice. The times are simulated.
32 devices in a mesh: groups: 2 (over y), expert: 16 (over z, x, core).
Axes of the slice: x: 2, y: 2, z: 4, core: 2. Of those that a mesh axis runs over, the one named last changes fastest.
Arguments:
- queries: bfloat16 [192, 6144], P(('groups', 'expert')), parts along dimension 0, may hold values from -8 to 8
- tree_key_value: bfloat16 [192, 2, 1024], P(('groups', 'expert')), parts along dimension 0, may hold values from -6 to 6
- key_value_cache: bfloat16 [32, 2, 512, 1024], P(('groups', 'expert')), parts along dimension 0, may hold values from -8 to 8
- lengths: int32 [32], P(('groups', 'expert')), parts along dimension 0, may hold values from 128 to 512, as said below
- parents: int32 [192], P(('groups', 'expert')), parts along dimension 0, may hold values from 0 to 4, as said below
- residual: bfloat16 [192, 6144], P(('groups', 'expert')), parts along dimension 0, may hold values from -6 to 6
- ffn_gain: bfloat16 [6144], replicated, may hold values from 0.099609375 to 1.8984375
- router: bfloat16 [6144, 4], replicated, may hold values from -0.078125 to 0.078125
- routes: int32 [192, 2], P(('groups', 'expert')), parts along dimension 0, may hold values from 0 to 3, all different within a row; in each aligned block of 6 rows (0 to 5, 6 to 11, ...) at most 4 rows name the same one
- gate_weight: bfloat16 [6144, 32768], P(None, 'expert'), may hold values from -0.078125 to 0.078125
- up_weight: bfloat16 [6144, 32768], P(None, 'expert'), may hold values from -0.078125 to 0.078125
- down_weight: bfloat16 [32768, 6144], P('expert'), may hold values from -0.0625 to 0.0625
- accepted: int32 [32], P(('groups', 'expert')), parts along dimension 0, may hold values from 0 to 5
- next_embed: bfloat16 [32, 6144], P(('groups', 'expert')), parts along dimension 0, may hold values from -6 to 6
- draft_fc: bfloat16 [12288, 6144], P('expert'), may hold values from -0.0546875 to 0.0546875
Outputs:
- layer_out: bfloat16 [192, 6144], P(('groups', 'expert')), parts along dimension 0
- draft_out: bfloat16 [32, 6144], P(('groups', 'expert')), parts along dimension 0
There are 2 independent parts, one for each index of `groups`. A program takes and returns all parts, laid end to end along the dimension named above; an argument that names none is the same for every part. Nothing has to cross between parts.
Inputs may be any that keep to these rules, and one draw needn't show every extreme that they name: `lengths`: both ends are reached by some request. `parents`: entry i of a request's 6 entries names an earlier node as its parent; entry 0, the root, names itself. `routes`: among the rows of one device no expert is named more than 4 times, a bound that some block reaches.
All inputs are finite; a program needn't handle non-finite values.
Results may differ from a plain program's by a relative error of at most 0.0051.
Values may be sent and summed in bfloat16 or wider, within the bound.
No kernel may reach another device: no remote copies, remote signals or barrier semaphores. Data moves between devices by JAX's collectives and lax.ppermute only.
A program may use at most 128 MiB of HBM per device.

v0:
```python
import jax
import jax.numpy as jnp
from jax import lax
from jax.sharding import PartitionSpec as P

QUERY_HEADS = 48
KEY_VALUE_HEADS = 8
HEAD_SIZE = 128
EXPERTS = 4
TREE_NODES = 6
CACHE_SLOTS = 512
CAP = 4


EPSILON = 1e-05


def ancestors(parent_ids):
    node_ids = jnp.arange(TREE_NODES, dtype=jnp.int32)
    parent_map = (parent_ids[:, :, None] == node_ids[None, None, :]).astype(jnp.float32)
    current = jnp.broadcast_to(jnp.eye(TREE_NODES, dtype=jnp.float32), parent_map.shape)
    reached = current
    for repeat in range(TREE_NODES):
        current = jnp.einsum("rij,rjk->rik", current, parent_map, precision=lax.Precision.HIGHEST)
        reached = reached + current
    return reached > 0.5


def attention(queries, tree_key_value, key_value_cache, lengths, parents):
    request_total = lengths.shape[0]
    query_head_count = queries.reshape(
        request_total, TREE_NODES, KEY_VALUE_HEADS, QUERY_HEADS // KEY_VALUE_HEADS, HEAD_SIZE
    )
    cached_key_rows = key_value_cache[:, 0].reshape(
        request_total, CACHE_SLOTS, KEY_VALUE_HEADS, HEAD_SIZE
    )
    cached_value_rows = key_value_cache[:, 1].reshape(
        request_total, CACHE_SLOTS, KEY_VALUE_HEADS, HEAD_SIZE
    )
    tree_key_rows = tree_key_value[:, 0].reshape(
        request_total, TREE_NODES, KEY_VALUE_HEADS, HEAD_SIZE
    )
    tree_value_rows = tree_key_value[:, 1].reshape(
        request_total, TREE_NODES, KEY_VALUE_HEADS, HEAD_SIZE
    )
    score_scale = HEAD_SIZE ** (-0.5)
    cache_scores = (
        jnp.einsum(
            "rtgqd,rlgd->rgtql",
            query_head_count,
            cached_key_rows,
            preferred_element_type=jnp.float32,
        )
        * score_scale
    )
    tree_scores = (
        jnp.einsum(
            "rtgqd,rugd->rgtqu", query_head_count, tree_key_rows, preferred_element_type=jnp.float32
        )
        * score_scale
    )
    visible = jnp.arange(CACHE_SLOTS, dtype=jnp.int32)[None, :] < lengths[:, None]
    related = ancestors(parents.reshape(request_total, TREE_NODES))
    cache_scores = jnp.where(visible[:, None, None, None, :], cache_scores, -1e30)
    tree_scores = jnp.where(related[:, None, :, None, :], tree_scores, -1e30)
    row_peak = jnp.maximum(jnp.max(cache_scores, axis=-1), jnp.max(tree_scores, axis=-1))[..., None]
    cache_exp = jnp.exp(cache_scores - row_peak)
    tree_exp = jnp.exp(tree_scores - row_peak)
    denominator = (jnp.sum(cache_exp, axis=-1) + jnp.sum(tree_exp, axis=-1))[..., None]
    cache_weights = (cache_exp / denominator).astype(jnp.bfloat16)
    tree_weights = (tree_exp / denominator).astype(jnp.bfloat16)
    context = jnp.einsum(
        "rgtql,rlgd->rtgqd", cache_weights, cached_value_rows, preferred_element_type=jnp.float32
    ) + jnp.einsum(
        "rgtqu,rugd->rtgqd", tree_weights, tree_value_rows, preferred_element_type=jnp.float32
    )
    return context.reshape(request_total * TREE_NODES, QUERY_HEADS * HEAD_SIZE)


def expert_rows(rows, gate_weight, up_weight, down_weight):
    gate_val = jnp.dot(rows, gate_weight, preferred_element_type=jnp.float32)
    up_val = jnp.dot(rows, up_weight, preferred_element_type=jnp.float32)
    activation = (jax.nn.silu(gate_val) * up_val).astype(jnp.bfloat16)
    return jnp.dot(activation, down_weight, preferred_element_type=jnp.float32).astype(jnp.bfloat16)


def per_device(
    queries,
    tree_key_value,
    key_value_cache,
    lengths,
    parents,
    residual,
    ffn_gain,
    router,
    routes,
    gate_weight,
    up_weight,
    down_weight,
    accepted,
    next_embed,
    draft_fc,
):
    devices = lax.axis_size("expert")
    group_size = devices // EXPERTS
    context = attention(queries, tree_key_value, key_value_cache, lengths, parents)
    hidden_state = residual.astype(jnp.float32) + context
    normed = (
        hidden_state
        * lax.rsqrt(jnp.mean(hidden_state * hidden_state, axis=-1, keepdims=True) + EPSILON)
        * ffn_gain.astype(jnp.float32)
    ).astype(jnp.bfloat16)
    tokens_here, model_width = normed.shape
    logits = jnp.dot(normed, router, preferred_element_type=jnp.float32)
    expert_ids = jnp.arange(EXPERTS, dtype=jnp.int32)
    first_hit = (routes[:, 0:1] == expert_ids[None, :]).astype(jnp.float32)
    second_hit = (routes[:, 1:2] == expert_ids[None, :]).astype(jnp.float32)
    first_logit = jnp.sum(logits * first_hit, axis=-1)
    second_logit = jnp.sum(logits * second_hit, axis=-1)
    first_share = jax.nn.sigmoid(first_logit - second_logit)
    mixing = first_share[:, None] * first_hit + (1.0 - first_share)[:, None] * second_hit
    hit_table = first_hit + second_hit
    slot_rank = jnp.cumsum(hit_table, axis=0) - 1.0
    slot_ids = jnp.arange(CAP, dtype=jnp.float32)
    placing = hit_table.T[:, None, :] * (slot_rank.T[:, None, :] == slot_ids[None, :, None]).astype(
        jnp.float32
    )
    packed = jnp.einsum(
        "ect,td->ecd", placing.astype(jnp.bfloat16), normed, preferred_element_type=jnp.float32
    ).astype(jnp.bfloat16)
    outgoing = jnp.broadcast_to(packed[:, None], (EXPERTS, group_size, CAP, model_width)).reshape(
        devices, CAP, model_width
    )
    received = lax.all_to_all(outgoing, "expert", split_axis=0, concat_axis=0, tiled=True)
    flat_rows = received.reshape(-1, model_width)
    computed = expert_rows(flat_rows, gate_weight, up_weight, down_weight).reshape(received.shape)
    returned = lax.all_to_all(computed, "expert", split_axis=0, concat_axis=0, tiled=True)
    grouped = jnp.sum(
        returned.reshape(EXPERTS, group_size, CAP, model_width), axis=1, dtype=jnp.float32
    )
    weighted = placing * mixing.T[:, None, :]
    expert_sum = jnp.einsum("ect,ecd->td", weighted, grouped, precision=lax.Precision.HIGHEST)
    layer_out = (hidden_state + expert_sum).astype(jnp.bfloat16)
    request_total = lengths.shape[0]
    picker = (accepted[:, None] == jnp.arange(TREE_NODES, dtype=jnp.int32)[None, :]).astype(
        jnp.bfloat16
    )
    picked = jnp.einsum(
        "rt,rtd->rd",
        picker,
        layer_out.reshape(request_total, TREE_NODES, model_width),
        preferred_element_type=jnp.float32,
    ).astype(jnp.bfloat16)
    draft_in = jnp.concatenate([picked, next_embed], axis=1)
    columns_in = lax.all_to_all(draft_in, "expert", split_axis=1, concat_axis=0, tiled=True)
    draft_out = lax.psum_scatter(
        jnp.dot(columns_in, draft_fc, preferred_element_type=jnp.float32),
        "expert",
        scatter_dimension=0,
        tiled=True,
    ).astype(jnp.bfloat16)
    return (layer_out, draft_out)


def solution(mesh):
    return jax.shard_map(
        per_device,
        mesh=mesh,
        in_specs=(
            P(("groups", "expert"), None),
            P(("groups", "expert"), None, None),
            P(("groups", "expert"), None, None, None),
            P(("groups", "expert")),
            P(("groups", "expert")),
            P(("groups", "expert"), None),
            P(),
            P(),
            P(("groups", "expert"), None),
            P(None, "expert"),
            P(None, "expert"),
            P("expert", None),
            P(("groups", "expert")),
            P(("groups", "expert"), None),
            P("expert", None),
        ),
        out_specs=(P(("groups", "expert"), None), P(("groups", "expert"), None)),
        check_vma=False,
    )
```

profile of v0, /device:TPU:0, one launch (start us, length us, event | category | flops | bytes accessed | tf_op | source)
XLA Modules:
  0.0 183.2 jit_solution(12144676580039937745)
XLA Ops:
  0.6 0.9 fusion.36
  1.5 0.8 fusion.35
  2.3 0.8 fusion.34
  3.2 0.8 fusion.33
  4.0 0.8 fusion.32
  4.9 0.8 fusion.6
  5.7 1.0 reshape.375
  6.7 0.9 slice_reduce_fusion
  7.7 1.7 fusion.50
  9.4 0.5 copy.71
  10.6 0.6 fusion.52
  12.0 0.5 copy.72
  12.8 0.5 fusion.5
  13.4 1.1 multiply_reduce_fusion
  14.5 0.7 convert_element_type.79
  15.2 0.8 slice_bitcast_fusion.1
  15.9 1.0 multiply_convert_fusion
  17.9 27.4 %all_to_all.23 = bf16[16,4,6144]{2,1,0:T(4,128)(2,1)S(1)} all-to-all(bf16[16,4,6144]{2,1,0:T(4,128)(2,1)S(1)} %bitcast.82), channel_id=1, replica_groups=mesh['groups'=2,'expert'=16] {'expert'}, dimensions={0} | all-to-all | bytes 1572864 | tf_op jit(solution)/shard_map/all_to_all | solution.py:134
  45.5 10.5 %fusion.53 = f32[64,2048]{1,0:T(8,128)S(1)} fusion(bf16[64,6144]{1,0:T(8,128)(2,1)S(1)} %reshape.382, bf16[6144,2048]{1,0:T(8,128)(2,1)} %param.24), kind=kOutput, calls=%fused_computation.97 | convolution fusion | flops 1610612736 | bytes 26476544 | tf_op jit(solution)/shard_map/dot_general | solution.py:81
  56.0 20.0 %convolution_convert_fusion = bf16[64,6144]{1,0:T(8,128)(2,1)S(1)} fusion(bf16[2048,6144]{1,0:T(8,128)(2,1)} %param.26, bf16[64,6144]{1,0:T(8,128)(2,1)S(1)} %reshape.382, bf16[6144,2048]{1,0:T(8,128)(2,1)} %param.25, f32[64,2048]{1,0:T(8,128)S(1)} %fusion.53), kind=kOutput, calls=%fused_computation | convolution fusion | flops 3222405120 | bytes 52428800 | tf_op jit(solution)/shard_map/dot_general | solution.py:84
  76.0 1.2 reshape.383
  77.2 3.9 %all-to-all-start.1 = ((bf16[16,4,6144]{2,1,0:T(4,128)(2,1)}), bf16[16,4,6144]{2,1,0:T(4,128)(2,1)S(1)}, u32[]{:S(2)}, u32[]{:S(2)}) async-start(bf16[16,4,6144]{2,1,0:T(4,128)(2,1)} %reshape.383), calls=%async_computation.1 | async-start | bytes 1572864 | tf_op jit(solution)/shard_map/all_to_all | solution.py:137
  81.8 17.9 %all-to-all-done.1 = bf16[16,4,6144]{2,1,0:T(4,128)(2,1)S(1)} async-done(((bf16[16,4,6144]{2,1,0:T(4,128)(2,1)}), bf16[16,4,6144]{2,1,0:T(4,128)(2,1)S(1)}, u32[]{:S(2)}, u32[]{:S(2)}) %all-to-all-start.1) | async-done | bytes 786464 | tf_op jit(solution)/shard_map/all_to_all | solution.py:137
  100.2 0.9 fusion.1
  101.9 0.8 reduce.13
  102.7 0.6 reshape.397
  103.3 5.5 %all-to-all-start.2 = ((bf16[16,2,384]{2,1,0:T(2,128)(2,1)}), bf16[16,2,384]{2,1,0:T(2,128)(2,1)S(1)}, u32[]{:S(2)}, u32[]{:S(2)}) async-start(bf16[16,2,384]{2,1,0:T(2,128)(2,1)} %reshape.397), calls=%async_computation.2 | async-start | bytes 49152 | tf_op jit(solution)/shard_map/all_to_all | solution.py:155
  108.8 0.7 dynamic-slice
  109.4 5.9 %all-to-all-done.2 = bf16[16,2,384]{2,1,0:T(2,128)(2,1)S(1)} async-done(((bf16[16,2,384]{2,1,0:T(2,128)(2,1)}), bf16[16,2,384]{2,1,0:T(2,128)(2,1)S(1)}, u32[]{:S(2)}, u32[]{:S(2)}) %all-to-all-start.2) | async-done | bytes 24608 | tf_op jit(solution)/shard_map/all_to_all | solution.py:155
  115.3 5.0 %fusion.22 = f32[16,6144]{1,0:T(8,128)S(1)} fusion(bf16[768,6144]{1,0:T(8,128)(2,1)} %param.29, bf16[1,16,768]{2,0,1:T(2,128)(2,1)S(1)} %bitcast.85), kind=kOutput, calls=%fused_computation.39 | convolution fusion | flops 150994944 | bytes 9854976 | tf_op jit(solution)/shard_map/dot_general | solution.py:157
  120.4 61.5 %all-reduce.2 = bf16[16,6144]{1,0:T(8,128)(2,1)S(1)} all-reduce(f32[16,6144]{1,0:T(8,128)S(1)} %fusion.22), channel_id=2, replica_groups=mesh['groups'=2,'expert'=16] {'expert'}, use_global_device_ids=true, to_apply=%region_9.10.clone | all-reduce | flops 98304 | bytes 589824
  181.9 1.3 dynamic-slice_convert_fusion
  (43 shorter events, 3.5 us)
Async XLA Ops:
  0.6 16.3 %copy-start = (bf16[6144,4]{0,1:T(4,128)(2,1)S(1)}, bf16[6144,4]{0,1:T(4,128)(2,1)}, u32[]{:S(2)}) copy-start(bf16[6144,4]{0,1:T(4,128)(2,1)} %param.22) | copy-start | bytes 147460
  56.0 25.8 %copy-start.4 = (bf16[1,6144]{1,0:T(2,128)(2,1)S(1)}, bf16[1,6144]{1,0:T(2,128)(2,1)}, u32[]{:S(2)}) copy-start(bf16[1,6144]{1,0:T(2,128)(2,1)} %param.28) | copy-start | bytes 36868
  56.0 44.2 %copy-start.2 = (bf16[6,6144]{1,0:T(8,128)(2,1)S(1)}, bf16[6,6144]{1,0:T(8,128)(2,1)}, u32[]{:S(2)}) copy-start(bf16[6,6144]{1,0:T(8,128)(2,1)} %param.20) | copy-start | bytes 221188
  56.0 52.8 %copy-start.5 = (u32[32]{0:T(128)S(1)}, u32[32]{0:T(128)}, u32[]{:S(2)}) copy-start(u32[32]{0:T(128)} %constant.42) | copy-start | bytes 388
  56.0 127.2 %copy-start.1 = (bf16[6144,4]{0,1:T(4,128)(2,1)S(1)}, bf16[6144,4]{0,1:T(4,128)(2,1)}, u32[]{:S(2)}) copy-start(bf16[6144,4]{0,1:T(4,128)(2,1)} %param.22) | copy-start | bytes 147460
  77.2 22.6 %all-to-all-start.1 = ((bf16[16,4,6144]{2,1,0:T(4,128)(2,1)}), bf16[16,4,6144]{2,1,0:T(4,128)(2,1)S(1)}, u32[]{:S(2)}, u32[]{:S(2)}) async-start(bf16[16,4,6144]{2,1,0:T(4,128)(2,1)} %reshape.383), calls=%async_computation.1 | async-start | bytes 1572864 | tf_op jit(solution)/shard_map/all_to_all | solution.py:137
  101.1 82.1 %copy-start.3 = (bf16[6,6144]{1,0:T(8,128)(2,1)}, bf16[6,6144]{1,0:T(8,128)(2,1)S(1)}, u32[]{:S(2)}) copy-start(bf16[6,6144]{1,0:T(8,128)(2,1)S(1)} %fusion.1) | copy-start | bytes 221188
  103.3 12.1 %all-to-all-start.2 = ((bf16[16,2,384]{2,1,0:T(2,128)(2,1)}), bf16[16,2,384]{2,1,0:T(2,128)(2,1)S(1)}, u32[]{:S(2)}, u32[]{:S(2)}) async-start(bf16[16,2,384]{2,1,0:T(2,128)(2,1)} %reshape.397), calls=%async_computation.2 | async-start | bytes 49152 | tf_op jit(solution)/shard_map/all_to_all | solution.py:155
where the time goes:
time: 184 us; the launch traced here: 183 us
  blocking collectives  88.9 us (48%)
  matrix products  43.7 us (24%)
  waiting for transfers between devices  23.8 us (13%)
  local copies, waits for them, and re-layouts  10.5 us (6%)
  starting transfers between devices  9.39 us (5%)
  other arithmetic  4.61 us (3%)
  between operations  2.26 us (1%)
    unnamed x1, blocking collectives  61.5 us
    all_to_all x1, blocking collectives, per_device(): lax.all_to_all(outgoing, 'expert', split_axis=0, concat_axis=0, tiled=True)  27.4 us
    dot_general x1, matrix products, expert_rows(): jnp.dot(activation, down_weight, preferred_element_type=jnp.float32)  20 us
    all_to_all x1, waiting for transfers between devices, per_device(): lax.all_to_all(computed, 'expert', split_axis=0, concat_axis=0, tiled=True)  17.9 us
    dot_general x1, matrix products, expert_rows(): gate_val = jnp.dot(rows, gate_weight, preferred_element_type=jnp.float32)  10.5 us
    all_to_all x1, waiting for transfers between devices, per_device(): lax.all_to_all(draft_in, 'expert', split_axis=1, concat_axis=0, tiled=True)  5.89 us
    all_to_all x1, starting transfers between devices, per_device(): lax.all_to_all(draft_in, 'expert', split_axis=1, concat_axis=0, tiled=True)  5.48 us
    dot_general x6, matrix products, ancestors(): jnp.einsum('rij,rjk->rik', current, parent_map, precision=lax.Precision.H...  5.08 us
  transfers between devices with their start and end apart: 2, of which 2 were waited for; matrix products, arithmetic and copies ran while one was open for 0% of the time, Pallas kernels for 0%

commit v1 on v0

--- a/solution.py
+++ b/solution.py
@@ -120,7 +120,9 @@
     first_share = jax.nn.sigmoid(first_logit - second_logit)
     mixing = first_share[:, None] * first_hit + (1.0 - first_share)[:, None] * second_hit
     hit_table = first_hit + second_hit
-    slot_rank = jnp.cumsum(hit_table, axis=0) - 1.0
+    row_ids = jnp.arange(tokens_here, dtype=jnp.int32)
+    earlier = (row_ids[None, :] < row_ids[:, None]).astype(jnp.float32)
+    slot_rank = jnp.sum(earlier[:, :, None] * hit_table[None, :, :], axis=1)
     slot_ids = jnp.arange(CAP, dtype=jnp.float32)
     placing = hit_table.T[:, None, :] * (slot_rank.T[:, None, :] == slot_ids[None, :, None]).astype(
         jnp.float32

time: 184 us -> 184 us (level)
  no operation moved by 1% of the time
where the time goes in v1:
time: 184 us; the launch traced here: 183 us
  blocking collectives  88.9 us (48%)
  matrix products  43.7 us (24%)
  waiting for transfers between devices  23.8 us (13%)
  local copies, waits for them, and re-layouts  10.6 us (6%)
  starting transfers between devices  9.39 us (5%)
  other arithmetic  4.52 us (2%)
  between operations  2.27 us (1%)
    unnamed x1, blocking collectives  61.5 us
    all_to_all x1, blocking collectives, per_device(): lax.all_to_all(outgoing, 'expert', split_axis=0, concat_axis=0, tiled=True)  27.4 us
    dot_general x1, matrix products, expert_rows(): jnp.dot(activation, down_weight, preferred_element_type=jnp.float32)  20 us
    all_to_all x1, waiting for transfers between devices, per_device(): lax.all_to_all(computed, 'expert', split_axis=0, concat_axis=0, tiled=True)  17.9 us
    dot_general x1, matrix products, expert_rows(): gate_val = jnp.dot(rows, gate_weight, preferred_element_type=jnp.float32)  10.5 us
    all_to_all x1, waiting for transfers between devices, per_device(): lax.all_to_all(draft_in, 'expert', split_axis=1, concat_axis=0, tiled=True)  5.89 us
    all_to_all x1, starting transfers between devices, per_device(): lax.all_to_all(draft_in, 'expert', split_axis=1, concat_axis=0, tiled=True)  5.47 us
    dot_general x6, matrix products, ancestors(): jnp.einsum('rij,rjk->rik', current, parent_map, precision=lax.Precision.H...  5.07 us
  transfers between devices with their start and end apart: 2, of which 2 were waited for; matrix products, arithmetic and copies ran while one was open for 0% of the time, Pallas kernels for 0%

profile of v1, /device:TPU:0, one launch (start us, length us, event | category | flops | bytes accessed | tf_op | source)
XLA Modules:
  0.0 183.2 jit_solution(16768544450189356391)
XLA Ops:
  0.7 0.8 fusion.36
  1.5 0.8 fusion.35
  2.3 0.8 fusion.34
  3.2 0.8 fusion.33
  4.0 0.8 fusion.32
  4.9 0.8 fusion.6
  5.7 1.0 reshape.431
  6.7 0.9 slice_reduce_fusion
  7.7 1.7 fusion.51
  9.4 0.5 copy.89
  10.6 0.6 fusion.53
  12.0 0.5 copy.90
  12.8 0.5 fusion.5
  13.4 1.1 multiply_reduce_fusion
  14.5 0.7 convert_element_type.95
  15.2 0.8 slice_bitcast_fusion.1
  15.9 1.0 multiply_convert_fusion
  17.9 27.4 %all_to_all.23 = bf16[16,4,6144]{2,1,0:T(4,128)(2,1)S(1)} all-to-all(bf16[16,4,6144]{2,1,0:T(4,128)(2,1)S(1)} %bitcast.81), channel_id=1, replica_groups=mesh['groups'=2,'expert'=16] {'expert'}, dimensions={0} | all-to-all | bytes 1572864 | tf_op jit(solution)/shard_map/all_to_all | solution.py:136
  45.5 10.5 %fusion.54 = f32[64,2048]{1,0:T(8,128)S(1)} fusion(bf16[64,6144]{1,0:T(8,128)(2,1)S(1)} %reshape.438, bf16[6144,2048]{1,0:T(8,128)(2,1)} %param.24), kind=kOutput, calls=%fused_computation.99 | convolution fusion | flops 1610612736 | bytes 26476544 | tf_op jit(solution)/shard_map/dot_general | solution.py:81
  56.0 20.0 %convolution_convert_fusion = bf16[64,6144]{1,0:T(8,128)(2,1)S(1)} fusion(bf16[2048,6144]{1,0:T(8,128)(2,1)} %param.26, bf16[64,6144]{1,0:T(8,128)(2,1)S(1)} %reshape.438, bf16[6144,2048]{1,0:T(8,128)(2,1)} %param.25, f32[64,2048]{1,0:T(8,128)S(1)} %fusion.54), kind=kOutput, calls=%fused_computation | convolution fusion | flops 3222405120 | bytes 52428800 | tf_op jit(solution)/shard_map/dot_general | solution.py:84
  76.0 1.2 reshape.439
  77.2 3.9 %all-to-all-start.1 = ((bf16[16,4,6144]{2,1,0:T(4,128)(2,1)}), bf16[16,4,6144]{2,1,0:T(4,128)(2,1)S(1)}, u32[]{:S(2)}, u32[]{:S(2)}) async-start(bf16[16,4,6144]{2,1,0:T(4,128)(2,1)} %reshape.439), calls=%async_computation.1 | async-start | bytes 1572864 | tf_op jit(solution)/shard_map/all_to_all | solution.py:139
  81.8 17.9 %all-to-all-done.1 = bf16[16,4,6144]{2,1,0:T(4,128)(2,1)S(1)} async-done(((bf16[16,4,6144]{2,1,0:T(4,128)(2,1)}), bf16[16,4,6144]{2,1,0:T(4,128)(2,1)S(1)}, u32[]{:S(2)}, u32[]{:S(2)}) %all-to-all-start.1) | async-done | bytes 786464 | tf_op jit(solution)/shard_map/all_to_all | solution.py:139
  100.2 0.9 fusion.1
  101.9 0.8 reduce.13
  102.6 0.6 reshape.453
  103.3 5.5 %all-to-all-start.2 = ((bf16[16,2,384]{2,1,0:T(2,128)(2,1)}), bf16[16,2,384]{2,1,0:T(2,128)(2,1)S(1)}, u32[]{:S(2)}, u32[]{:S(2)}) async-start(bf16[16,2,384]{2,1,0:T(2,128)(2,1)} %reshape.453), calls=%async_computation.2 | async-start | bytes 49152 | tf_op jit(solution)/shard_map/all_to_all | solution.py:157
  108.8 0.7 dynamic-slice
  109.4 5.9 %all-to-all-done.2 = bf16[16,2,384]{2,1,0:T(2,128)(2,1)S(1)} async-done(((bf16[16,2,384]{2,1,0:T(2,128)(2,1)}), bf16[16,2,384]{2,1,0:T(2,128)(2,1)S(1)}, u32[]{:S(2)}, u32[]{:S(2)}) %all-to-all-start.2) | async-done | bytes 24608 | tf_op jit(solution)/shard_map/all_to_all | solution.py:157
  115.3 5.0 %fusion.22 = f32[16,6144]{1,0:T(8,128)S(1)} fusion(bf16[768,6144]{1,0:T(8,128)(2,1)} %param.29, bf16[1,16,768]{2,0,1:T(2,128)(2,1)S(1)} %bitcast.84), kind=kOutput, calls=%fused_computation.39 | convolution fusion | flops 150994944 | bytes 9854976 | tf_op jit(solution)/shard_map/dot_general | solution.py:159
  120.4 61.5 %all-reduce.2 = bf16[16,6144]{1,0:T(8,128)(2,1)S(1)} all-reduce(f32[16,6144]{1,0:T(8,128)S(1)} %fusion.22), channel_id=2, replica_groups=mesh['groups'=2,'expert'=16] {'expert'}, use_global_device_ids=true, to_apply=%region_9.10.clone | all-reduce | flops 98304 | bytes 589824
  181.8 1.3 dynamic-slice_convert_fusion
  (44 shorter events, 3.5 us)
Async XLA Ops:
  0.6 16.3 %copy-start = (bf16[6144,4]{0,1:T(4,128)(2,1)S(1)}, bf16[6144,4]{0,1:T(4,128)(2,1)}, u32[]{:S(2)}) copy-start(bf16[6144,4]{0,1:T(4,128)(2,1)} %param.22) | copy-start | bytes 147460
  55.9 25.8 %copy-start.4 = (bf16[1,6144]{1,0:T(2,128)(2,1)S(1)}, bf16[1,6144]{1,0:T(2,128)(2,1)}, u32[]{:S(2)}) copy-start(bf16[1,6144]{1,0:T(2,128)(2,1)} %param.28) | copy-start | bytes 36868
  56.0 44.2 %copy-start.2 = (bf16[6,6144]{1,0:T(8,128)(2,1)S(1)}, bf16[6,6144]{1,0:T(8,128)(2,1)}, u32[]{:S(2)}) copy-start(bf16[6,6144]{1,0:T(8,128)(2,1)} %param.20) | copy-start | bytes 221188
  56.0 52.8 %copy-start.5 = (u32[32]{0:T(128)S(1)}, u32[32]{0:T(128)}, u32[]{:S(2)}) copy-start(u32[32]{0:T(128)} %constant.36) | copy-start | bytes 388
  56.0 127.2 %copy-start.1 = (bf16[6144,4]{0,1:T(4,128)(2,1)S(1)}, bf16[6144,4]{0,1:T(4,128)(2,1)}, u32[]{:S(2)}) copy-start(bf16[6144,4]{0,1:T(4,128)(2,1)} %param.22) | copy-start | bytes 147460
  77.2 22.6 %all-to-all-start.1 = ((bf16[16,4,6144]{2,1,0:T(4,128)(2,1)}), bf16[16,4,6144]{2,1,0:T(4,128)(2,1)S(1)}, u32[]{:S(2)}, u32[]{:S(2)}) async-start(bf16[16,4,6144]{2,1,0:T(4,128)(2,1)} %reshape.439), calls=%async_computation.1 | async-start | bytes 1572864 | tf_op jit(solution)/shard_map/all_to_all | solution.py:139
  101.1 82.1 %copy-start.3 = (bf16[6,6144]{1,0:T(8,128)(2,1)}, bf16[6,6144]{1,0:T(8,128)(2,1)S(1)}, u32[]{:S(2)}) copy-start(bf16[6,6144]{1,0:T(8,128)(2,1)S(1)} %fusion.1) | copy-start | bytes 221188
  103.3 12.0 %all-to-all-start.2 = ((bf16[16,2,384]{2,1,0:T(2,128)(2,1)}), bf16[16,2,384]{2,1,0:T(2,128)(2,1)S(1)}, u32[]{:S(2)}, u32[]{:S(2)}) async-start(bf16[16,2,384]{2,1,0:T(2,128)(2,1)} %reshape.453), calls=%async_computation.2 | async-start | bytes 49152 | tf_op jit(solution)/shard_map/all_to_all | solution.py:157

commit v2 on v0

v2 whole, which is shorter than its diff:
```python
import functools
import jax
import jax.numpy as jnp
from jax import lax
from jax.experimental import pallas as pl
from jax.experimental.pallas import tpu as pltpu
from jax.sharding import PartitionSpec as P

QUERY_HEADS = 48
KEY_VALUE_HEADS = 8
HEAD_SIZE = 128
EXPERTS = 4
TREE_NODES = 6
CAP = 4
ROWS = 8
LANES = 128
EPSILON = 1e-05
HIDDEN = -1e30

F32 = jnp.float32
BF16 = jnp.bfloat16
VMEM = pltpu.VMEM
SMEM = pltpu.SMEM
MIB = 1 << 20


def spec(space):
    return pl.BlockSpec(memory_space=space)


def iota(shape, axis):
    return lax.broadcasted_iota(jnp.int32, shape, axis)


def along(values, shape, axis, fill=-1):
    index = iota(shape, axis)
    out = jnp.full(shape, fill, jnp.int32)
    for at, value in enumerate(values):
        out = jnp.where(index == at, value, out)
    return out


def attend(
    per_expert,
    draft_cols,
    lengths,
    parents,
    routes,
    accepted,
    queries_far,
    tree_far,
    cache,
    residual_far,
    gain_far,
    router_far,
    embed_far,
    gate,
    up,
    hidden_out,
    payload,
    placing_out,
    gate_first,
    up_first,
    queries,
    tree_key_value,
    keys,
    values,
    residual,
    gain,
    router,
    embed,
    tree,
    padded,
    hidden,
    sems,
):
    width = queries.shape[1]
    chips = payload.shape[0]
    shared = QUERY_HEADS // KEY_VALUE_HEADS
    first = gate_first.shape[1]
    moves = [
        (queries_far, queries),
        (tree_far, tree_key_value),
        (cache.at[0, 0], keys),
        (cache.at[0, 1], values),
        (residual_far, residual),
        (gain_far, gain),
        (router_far, router),
        (embed_far, embed),
        (gate.at[:, pl.ds(0, first)], gate_first),
        (up.at[:, pl.ds(0, first)], up_first),
    ]
    copies = [
        pltpu.make_async_copy(source, target, sems.at[i])
        for i, (source, target) in enumerate(moves)
    ]
    for copy in copies:
        copy.start()

    bits = []
    for t in range(TREE_NODES):
        above = jnp.int32(0)
        for j in range(t):
            above = jnp.where(parents[t] == j, bits[j], above)
        bits.append(above | (1 << t))
    counts = [jnp.int32(0)] * EXPERTS
    slots = [[], []]
    for t in range(TREE_NODES):
        for k in range(2):
            slot = jnp.int32(0)
            for e in range(EXPERTS):
                slot = jnp.where(routes[k, t] == e, e * CAP + counts[e], slot)
            slots[k].append(slot)
        for e in range(EXPERTS):
            named = jnp.logical_or(routes[0, t] == e, routes[1, t] == e)
            counts[e] = counts[e] + named.astype(jnp.int32)

    tree[...] = jnp.zeros(tree.shape, F32)
    copies[0].wait()
    copies[1].wait()
    for t in range(TREE_NODES):
        pair = tree_key_value[t].astype(F32)
        tree[0, t : t + 1, :] = pair[0:1]
        tree[1, t : t + 1, :] = pair[1:2]
    padded[...] = jnp.zeros(padded.shape, F32)
    padded[0:TREE_NODES, :] = queries[...].astype(F32)

    slots_total = keys.shape[0]
    visible = iota((shared * ROWS, slots_total), 1) < lengths[0]
    row = iota((shared * ROWS, ROWS), 0) & (ROWS - 1)
    row_bits = jnp.ones((shared * ROWS, ROWS), jnp.int32)
    for t in range(TREE_NODES):
        row_bits = jnp.where(row == t, bits[t], row_bits)
    related = ((row_bits >> iota((shared * ROWS, ROWS), 1)) & 1) == 1
    scale = HEAD_SIZE ** (-0.5)
    contract_last = (((1,), (1,)), ((), ()))
    for copy in copies[2:8]:
        copy.wait()
    hidden[...] = jnp.zeros(hidden.shape, F32)
    hidden[0:TREE_NODES, :] = residual[...].astype(F32)
    for g in range(KEY_VALUE_HEADS):
        head = slice(g * HEAD_SIZE, (g + 1) * HEAD_SIZE)
        block = jnp.concatenate(
            [
                padded[:, (g * shared + i) * HEAD_SIZE : (g * shared + i + 1) * HEAD_SIZE]
                for i in range(shared)
            ],
            axis=0,
        ).astype(BF16)
        cache_scores = (
            lax.dot_general(block, keys[:, head], contract_last, preferred_element_type=F32)
            * scale
        )
        tree_scores = (
            lax.dot_general(
                block, tree[0, :, head].astype(BF16), contract_last, preferred_element_type=F32
            )
            * scale
        )
        cache_scores = jnp.where(visible, cache_scores, HIDDEN)
        tree_scores = jnp.where(related, tree_scores, HIDDEN)
        peak = jnp.maximum(
            jnp.max(cache_scores, axis=1, keepdims=True),
            jnp.max(tree_scores, axis=1, keepdims=True),
        )
        cache_exp = jnp.exp(cache_scores - peak)
        tree_exp = jnp.exp(tree_scores - peak)
        total = jnp.sum(cache_exp, axis=1, keepdims=True) + jnp.sum(
            tree_exp, axis=1, keepdims=True
        )
        share = 1.0 / total
        context = jnp.dot(
            (cache_exp * share).astype(BF16), values[:, head], preferred_element_type=F32
        ) + jnp.dot(
            (tree_exp * share).astype(BF16),
            tree[1, :, head].astype(BF16),
            preferred_element_type=F32,
        )
        for i in range(shared):
            columns = slice((g * shared + i) * HEAD_SIZE, (g * shared + i + 1) * HEAD_SIZE)
            hidden[:, columns] = hidden[:, columns] + context[i * ROWS : (i + 1) * ROWS]

    state = hidden[...]
    hidden_out[...] = state
    mean = jnp.sum(state * state, axis=1, keepdims=True) * (1.0 / width)
    gains = gain[...].astype(F32)
    shrink = lax.rsqrt(mean + EPSILON)
    normed = jnp.concatenate(
        [
            state[:, i * LANES : (i + 1) * LANES] * shrink * gains[i : i + 1]
            for i in range(width // LANES)
        ],
        axis=1,
    ).astype(BF16)
    logits = lax.dot_general(normed, router[...], contract_last, preferred_element_type=F32)
    expert = iota((ROWS, EXPERTS), 1)
    route = [
        along([routes[k, t] for t in range(TREE_NODES)], (ROWS, EXPERTS), 0) for k in range(2)
    ]
    picked_logit = [
        jnp.sum(jnp.where(expert == route[k], logits, 0.0), axis=1, keepdims=True)
        for k in range(2)
    ]
    first = jax.nn.sigmoid(picked_logit[0] - picked_logit[1])
    lane = iota((ROWS, LANES), 1)
    is_accepted = (iota((ROWS, LANES), 0) == accepted[0]).astype(F32)
    extras = []
    for weight in (first, 1.0 - first):
        high = weight.astype(BF16).astype(F32)
        extras.append(
            jnp.where(
                lane == 0,
                high,
                jnp.where(lane == 1, weight - high, jnp.where(lane == 2, is_accepted, 0.0)),
            ).astype(BF16)
        )
    place_row = iota((EXPERTS * ROWS, ROWS), 0)
    target = (place_row // ROWS) * CAP + (place_row & (ROWS - 1))
    target = jnp.where((place_row & (ROWS - 1)) < CAP, target, -2)
    hits = [
        (target == along(slots[k], (EXPERTS * ROWS, ROWS), 1)).astype(F32).astype(BF16)
        for k in range(2)
    ]
    packed = jnp.dot(hits[0] + hits[1], normed, preferred_element_type=F32)
    extra = jnp.dot(hits[0], extras[0], preferred_element_type=F32) + jnp.dot(
        hits[1], extras[1], preferred_element_type=F32
    )
    for e in range(EXPERTS):
        rows = packed[e * ROWS : e * ROWS + CAP].astype(BF16)
        last = extra[e * ROWS : e * ROWS + CAP].astype(BF16)
        for q in range(e * per_expert, (e + 1) * per_expert):
            payload[q, :, 0:width] = rows
            payload[q, :, payload.shape[2] - LANES :] = last
    if draft_cols:
        chosen = jnp.sum(
            jnp.where(iota((ROWS, width), 0) == accepted[0], state, 0.0), axis=0, keepdims=True
        )
        rest = embed[...].astype(F32)
        for q in range(chips):
            for i in range(CAP):
                at = (q * CAP + i) * draft_cols
                source = chosen if at < width else rest
                at = at % width
                payload[q, i : i + 1, width : width + draft_cols] = source[
                    :, at : at + draft_cols
                ].astype(BF16)
    lane_slot = iota(placing_out.shape, 1)
    lane_slot = (lane_slot // (CAP * per_expert)) * CAP + lane_slot % CAP
    placing_out[...] = jnp.logical_or(
        lane_slot == along(slots[0], placing_out.shape, 0),
        lane_slot == along(slots[1], placing_out.shape, 0),
    ).astype(F32)
    for copy in copies[8:]:
        copy.wait()


def experts(
    width,
    mine,
    other,
    gate_first,
    up_first,
    gate,
    up,
    down,
    keep,
    send,
    notes,
    weights,
    rows,
    acts,
    gates,
    ups,
    downs,
    gate_sems,
    up_sems,
    down_sems,
):
    chips, _, whole_width = mine.shape
    half = chips * CAP
    first = gate_first.shape[1]
    buffers, _, chunk = gates.shape
    down_buffers, hidden_units, step = downs.shape
    chunks = (hidden_units - first) // chunk
    steps = width // step

    def gate_copies(i):
        columns = pl.ds(first + i * chunk, chunk)
        slot = i % buffers
        return (
            pltpu.make_async_copy(gate.at[:, columns], gates.at[slot], gate_sems.at[slot]),
            pltpu.make_async_copy(up.at[:, columns], ups.at[slot], up_sems.at[slot]),
        )

    def down_copy(i):
        slot = i % down_buffers
        return pltpu.make_async_copy(
            down.at[:, pl.ds(i * step, step)], downs.at[slot], down_sems.at[slot]
        )

    queue = [copy for i in range(chunks) for copy in gate_copies(i)]
    queue += [down_copy(i) for i in range(steps)]
    ahead = 2 * buffers

    def issue(upto):
        nonlocal issued
        while issued < min(upto, len(queue)):
            queue[issued].start()
            issued += 1

    issued = 0
    issue(ahead)
    group = 16 // CAP
    for side, source in enumerate((mine, other)):
        for q in range(0, chips, group):
            at = slice(side * half + q * CAP, side * half + (q + group) * CAP)
            full = jnp.concatenate(
                [source[q + i].astype(F32) for i in range(group)], axis=0
            )
            rows[at, :] = full[:, 0:width].astype(BF16)
            notes[at, :] = full[:, width : whole_width - LANES].astype(BF16)
            weights[at, :] = full[:, whole_width - LANES :]

    def activate(gate_block, up_block, at):
        gate_val = jnp.dot(rows[...], gate_block, preferred_element_type=F32)
        up_val = jnp.dot(rows[...], up_block, preferred_element_type=F32)
        acts[:, at : at + gate_block.shape[1]] = (
            gate_val / (1.0 + jnp.exp(-gate_val)) * up_val
        ).astype(BF16)

    for at in range(0, first, chunk):
        activate(gate_first[:, at : at + chunk], up_first[:, at : at + chunk], at)
    for i in range(chunks):
        for copy in gate_copies(i):
            copy.wait()
        slot = i % buffers
        activate(gates[slot], ups[slot], first + i * chunk)
        if i + buffers < chunks:
            issue(ahead + 2 * (i + 1))
        else:
            issue(2 * chunks + (i + buffers - chunks + 1) * down_buffers // buffers)
    mix = weights[:, 0:1] + weights[:, 1:2]
    for i in range(steps):
        down_copy(i).wait()
        result = jnp.dot(acts[...], downs[i % down_buffers], preferred_element_type=F32) * mix
        columns = slice(i * step, (i + 1) * step)
        keep[:, columns] = result[:half]
        send[:, columns] = result[half:].astype(BF16)
        issue(2 * chunks + down_buffers + i + 1)


def combine(draft_cols, keep, came, flags, returned, draft):
    chips = returned.shape[0]
    width = keep.shape[1]
    total = keep[...] + came[...].astype(F32)
    for q in range(chips):
        returned[q] = total[q * CAP : (q + 1) * CAP].astype(BF16)
    row = iota((chips * CAP, chips), 0)
    select = jnp.where(row // CAP == iota((chips * CAP, chips), 1), flags[0 : chips * CAP, 2:3], 0.0)
    chosen = lax.dot_general(
        select.astype(BF16),
        total.astype(BF16),
        (((0,), (0,)), ((), ())),
        preferred_element_type=F32,
    ).astype(BF16)
    if draft_cols:
        for d in range(draft.shape[0]):
            if d * draft_cols < width:
                draft[d] = chosen[:, d * draft_cols : (d + 1) * draft_cols]
            else:
                draft[d] = jnp.zeros(draft.shape[1:], BF16)
    else:
        draft[...] = chosen


def project(came, notes, fc, out, near, spread, sems):
    devices, requests, columns = came.shape
    chips = devices // 2
    half = chips * CAP
    pieces, step = out.shape[1:]
    copies = [
        pltpu.make_async_copy(
            fc.at[:, pl.ds(i * step, step)], near.at[:, pl.ds(i * step, step)], sems.at[i]
        )
        for i in range(pieces)
    ]
    for copy in copies:
        copy.start()
    core = lax.axis_index("expert") % 2
    row = iota((chips, half), 0)
    col = iota((chips, half), 1)
    sides = []
    for side in range(2):
        stacked = notes[side * half : (side + 1) * half, : 2 * columns // CAP]
        flat = jnp.concatenate(
            [
                jnp.dot(
                    (col == row * CAP + i).astype(F32).astype(BF16),
                    stacked,
                    preferred_element_type=F32,
                )
                for i in range(CAP)
            ],
            axis=1,
        )
        sides.append(jnp.where(core == 0, flat[:, :columns], flat[:, columns:]))
    inputs = []
    for c in range(2):
        total = jnp.where(core == 0, sides[c], sides[1 - c])
        for q in range(chips):
            total = total + came[2 * q + c].astype(F32)
        inputs.append(total)
    inputs = jnp.concatenate(inputs, axis=0).astype(BF16)
    for i in range(pieces):
        copies[i].wait()
        result = jnp.dot(
            inputs, near[:, i * step : (i + 1) * step], preferred_element_type=F32
        )
        for k in range(step // LANES):
            spread[k, pl.ds(i, devices, stride=pieces), :] = result[
                :, k * LANES : (k + 1) * LANES
            ]
    for c in range(2):
        for q in range(chips):
            at = (c * chips + q) * pieces
            for k in range(step // LANES):
                out[2 * q + c, :, k * LANES : (k + 1) * LANES] = spread[
                    k, at : at + pieces, :
                ].astype(BF16)


def finish(came, out):
    total = came[0].astype(F32)
    for d in range(1, came.shape[0]):
        total = total + came[d].astype(F32)
    step = total.shape[1]
    for i in range(total.shape[0]):
        out[:, i * step : (i + 1) * step] = total[i : i + 1].astype(BF16)


def settle(hidden, placing, came, out):
    chips = came.shape[0]
    rows = jnp.concatenate([came[q].astype(F32) for q in range(chips)], axis=0).astype(BF16)
    total = hidden[...] + jnp.dot(
        placing[...].astype(BF16), rows, preferred_element_type=F32
    )
    out[...] = total[: out.shape[0]].astype(BF16)


def far(array):
    return pltpu.with_memory_space_constraint(array, pltpu.HBM)


def near(array):
    return pltpu.with_memory_space_constraint(array, VMEM)


def params(mib):
    return pltpu.CompilerParams(vmem_limit_bytes=mib * MIB)


def per_device(
    queries,
    tree_key_value,
    key_value_cache,
    lengths,
    parents,
    residual,
    ffn_gain,
    router,
    routes,
    gate_weight,
    up_weight,
    down_weight,
    accepted,
    next_embed,
    draft_fc,
):
    devices = lax.axis_size("expert")
    chips = devices // 2
    per_expert = chips // EXPERTS
    tokens, width = queries.shape
    assert lengths.shape[0] == 1 and tokens == TREE_NODES
    cache_slots, key_width = key_value_cache.shape[2:]
    hidden_units = gate_weight.shape[1]
    draft_rows = draft_fc.shape[0]
    aligned = (2 * draft_rows) % (CAP * LANES) == 0
    ext = 2 * draft_rows // CAP
    ext_pad = -(-ext // LANES) * LANES
    total_width = width + ext_pad + LANES
    same_core = [[2 * q + c for q in range(chips)] for c in range(2)]
    swap = [(d, d ^ 1) for d in range(devices)]

    first = 512 if hidden_units > 1024 else hidden_units // 2
    chunk = min(256, first)
    hidden, payload, placing, gate_first, up_first = pl.pallas_call(
        functools.partial(attend, per_expert, ext if aligned else 0),
        out_shape=(
            jax.ShapeDtypeStruct((ROWS, width), F32),
            jax.ShapeDtypeStruct((chips, CAP, total_width), BF16),
            jax.ShapeDtypeStruct((ROWS, chips * CAP), F32),
            VMEM((width, first), BF16),
            VMEM((width, first), BF16),
        ),
        in_specs=[spec(SMEM)] * 4 + [spec(pl.ANY)] * 9,
        out_specs=(spec(VMEM),) * 5,
        scratch_shapes=[
            VMEM(queries.shape, BF16),
            VMEM(tree_key_value.shape, BF16),
            VMEM((cache_slots, key_width), BF16),
            VMEM((cache_slots, key_width), BF16),
            VMEM(residual.shape, BF16),
            VMEM((width // LANES, LANES), BF16),
            VMEM((EXPERTS, width), BF16),
            VMEM(next_embed.shape, BF16),
            VMEM((2, ROWS, key_width), F32),
            VMEM((ROWS, width), F32),
            VMEM((ROWS, width), F32),
            pltpu.SemaphoreType.DMA((10,)),
        ],
        compiler_params=params(12),
    )(
        lengths,
        parents,
        routes.T,
        accepted,
        far(queries),
        far(tree_key_value),
        far(key_value_cache),
        far(residual),
        far(ffn_gain.reshape(width // LANES, LANES)),
        far(router.T),
        far(next_embed),
        far(gate_weight),
        far(up_weight),
    )
    if not aligned:
        chosen = lax.dynamic_slice_in_dim(hidden, accepted[0], 1, 0)
        early_cols = jnp.concatenate([chosen.astype(BF16), next_embed], axis=1)
        early_cols = early_cols.reshape(chips, CAP, ext)
        early_cols = jnp.pad(early_cols, ((0, 0), (0, 0), (0, ext_pad - ext)))
        payload = lax.dynamic_update_slice(payload, early_cols, (0, 0, width))

    mine = lax.all_to_all(
        payload, "expert", 0, 0, tiled=True, axis_index_groups=same_core
    )
    other = lax.ppermute(mine, "expert", swap)
    step = 512
    buffers, down_buffers = 3, 6
    rows = 2 * chips * CAP
    keep, send, notes, weights = pl.pallas_call(
        functools.partial(experts, width),
        out_shape=(
            VMEM((chips * CAP, width), F32),
            VMEM((chips * CAP, width), BF16),
            VMEM((rows, ext_pad), BF16),
            VMEM((rows, LANES), F32),
        ),
        in_specs=[spec(VMEM)] * 4 + [spec(pl.ANY)] * 3,
        out_specs=(spec(VMEM),) * 4,
        scratch_shapes=[
            VMEM((rows, width), BF16),
            VMEM((rows, hidden_units), BF16),
            VMEM((buffers, width, chunk), BF16),
            VMEM((buffers, width, chunk), BF16),
            VMEM((down_buffers, hidden_units, step), BF16),
            pltpu.SemaphoreType.DMA((buffers,)),
            pltpu.SemaphoreType.DMA((buffers,)),
            pltpu.SemaphoreType.DMA((down_buffers,)),
        ],
        compiler_params=params(40),
        cost_estimate=pl.CostEstimate(
            flops=2 * rows * width * hidden_units * 3,
            bytes_accessed=3 * down_weight.size * 2,
            transcendentals=0,
        ),
    )(
        near(mine),
        near(other),
        near(gate_first),
        near(up_first),
        far(gate_weight),
        far(up_weight),
        far(down_weight),
    )
    came = lax.ppermute(send, "expert", swap)
    draft_shape = (devices, chips, draft_rows) if aligned else (chips, width)
    partial, draft = pl.pallas_call(
        functools.partial(combine, draft_rows if aligned else 0),
        out_shape=(
            jax.ShapeDtypeStruct((chips, CAP, width), BF16),
            jax.ShapeDtypeStruct(draft_shape, BF16),
        ),
        in_specs=[spec(VMEM)] * 3,
        out_specs=(spec(VMEM),) * 2,
        compiler_params=params(12 if aligned else 40),
    )(near(keep), came, near(weights))
    if not aligned:
        draft = draft.reshape(chips, devices // 2, draft_rows).transpose(1, 0, 2)
        draft = jnp.concatenate([draft, jnp.zeros_like(draft)], axis=0)
    draft_came = lax.all_to_all(draft, "expert", 0, 0, tiled=True)
    returned = lax.all_to_all(
        partial, "expert", 0, 0, tiled=True, axis_index_groups=same_core
    )
    sums = pl.pallas_call(
        project,
        out_shape=jax.ShapeDtypeStruct((devices, ROWS, width // ROWS), BF16),
        in_specs=[spec(VMEM)] * 2 + [spec(pl.ANY)],
        out_specs=spec(VMEM),
        scratch_shapes=[
            VMEM(draft_fc.shape, BF16),
            VMEM((width // ROWS // LANES, devices * ROWS, LANES), F32),
            pltpu.SemaphoreType.DMA((ROWS,)),
        ],
        compiler_params=params(24),
    )(draft_came, notes, far(draft_fc))
    sums_came = lax.all_to_all(sums, "expert", 0, 0, tiled=True)
    layer_out = pl.pallas_call(
        settle,
        out_shape=jax.ShapeDtypeStruct((tokens, width), BF16),
        in_specs=[spec(VMEM)] * 3,
        out_specs=spec(VMEM),
        compiler_params=params(16),
    )(hidden, placing, returned)
    draft_out = pl.pallas_call(
        finish,
        out_shape=jax.ShapeDtypeStruct((1, width), BF16),
        in_specs=[spec(VMEM)],
        out_specs=spec(VMEM),
        compiler_params=params(8),
    )(sums_came)
    return (layer_out, draft_out)


def solution(mesh):
    return jax.shard_map(
        per_device,
        mesh=mesh,
        in_specs=(
            P(("groups", "expert"), None),
            P(("groups", "expert"), None, None),
            P(("groups", "expert"), None, None, None),
            P(("groups", "expert")),
            P(("groups", "expert")),
            P(("groups", "expert"), None),
            P(),
            P(),
            P(("groups", "expert"), None),
            P(None, "expert"),
            P(None, "expert"),
            P("expert", None),
            P(("groups", "expert")),
            P(("groups", "expert"), None),
            P("expert", None),
        ),
        out_specs=(P(("groups", "expert"), None), P(("groups", "expert"), None)),
        check_vma=False,
    )
```

time: 184 us -> 96.4 us (0.52)
  blocking collectives: 88.9 us -> 32 us
  matrix products: 43.7 us -> 0 us
  Pallas kernels: 0 us -> 34.9 us
  local copies, waits for them, and re-layouts: 10.5 us -> 1.33 us
  waiting for transfers between devices: 23.8 us -> 18.4 us
  other arithmetic: 4.61 us -> 0 us
  starting transfers between devices: 9.39 us -> 7.38 us
    unnamed x1 -> x0, blocking collectives: 61.5 us -> none
    dot_general x17 -> x0, matrix products: 43.7 us -> none  [the longest x1 20 us: expert_rows(): jnp.dot(activation, down_weight, preferred_element_type=jnp.float32)]
    pallas_call x0 -> x6, Pallas kernels: none -> 34.9 us  [the longest x1 21.6 us: per_device(): pl.pallas_call(functools.partial(experts, width), out_shape=(VMEM((chips...]
    all_to_all x2, waiting for transfers between devices: 23.8 us -> 15.1 us  [the longest x1 8.13 us: per_device(): sums_came = lax.all_to_all(sums, 'expert', 0, 0, tiled=True)]
    all_to_all x1 -> x2, blocking collectives: 27.4 us -> 32 us  [the longest x1 19.7 us: per_device(): lax.all_to_all(payload, 'expert', 0, 0, tiled=True, axis_index_groups=sam...]
    ppermute x0 -> x2, waiting for transfers between devices: none -> 3.35 us  [the longest x1 1.77 us: per_device(): other = lax.ppermute(mine, 'expert', swap)]
    slice x2 -> x0, local copies, waits for them, and re-layouts: 2.65 us -> none  [the longest x1 1.72 us: attention(): key_value_cache[:, 1]]
    all_to_all x2, starting transfers between devices: 9.39 us -> 7.17 us  [the longest x1 3.72 us: per_device(): sums_came = lax.all_to_all(sums, 'expert', 0, 0, tiled=True)]
  transfers between devices with their start and end apart: 2 -> 4, of which waited for: 2 -> 4; matrix products, arithmetic and copies ran while one was open for 0% -> 0% of each run, Pallas kernels for 0% -> 6%
where the time goes in v2:
time: 96.4 us; the launch traced here: 96 us
  Pallas kernels  34.9 us (36%)
  blocking collectives  32 us (33%)
  waiting for transfers between devices  18.4 us (19%)
  starting transfers between devices  7.38 us (8%)
  between operations  1.98 us (2%)
  local copies, waits for them, and re-layouts  1.33 us (1%)
    pallas_call x1, Pallas kernels, per_device(): pl.pallas_call(functools.partial(experts, width), out_shape=(VMEM((chips...  21.6 us
    all_to_all x1, blocking collectives, per_device(): lax.all_to_all(payload, 'expert', 0, 0, tiled=True, axis_index_groups=sam...  19.7 us
    all_to_all x1, blocking collectives, per_device(): draft_came = lax.all_to_all(draft, 'expert', 0, 0, tiled=True)  12.2 us
    all_to_all x1, waiting for transfers between devices, per_device(): sums_came = lax.all_to_all(sums, 'expert', 0, 0, tiled=True)  8.13 us
    all_to_all x1, waiting for transfers between devices, per_device(): lax.all_to_all(partial, 'expert', 0, 0, tiled=True, axis_index_groups=sam...  6.93 us
    pallas_call x1, Pallas kernels, per_device(): pl.pallas_call(functools.partial(attend, per_expert, ext if aligned else...  6.01 us
    pallas_call x1, Pallas kernels, per_device(): pl.pallas_call(project, out_shape=jax.ShapeDtypeStruct((devices, ROWS, wi...  4.84 us
    all_to_all x1, starting transfers between devices, per_device(): sums_came = lax.all_to_all(sums, 'expert', 0, 0, tiled=True)  3.72 us
  transfers between devices with their start and end apart: 4, of which 4 were waited for; matrix products, arithmetic and copies ran while one was open for 0% of the time, Pallas kernels for 6%

profile of v2, /device:TPU:0, one launch (start us, length us, event | category | flops | bytes accessed | tf_op | source)
XLA Modules:
  0.0 96.0 jit_solution(81024080017315742)
XLA Ops:
  1.9 0.0 copy-start
  1.9 0.7 copy-done
  2.6 0.0 copy-start.1
  2.6 0.7 copy-done.1
  3.3 6.0 %shard_map.158 = (f32[8,6144]{1,0:T(8,128)S(1)}, bf16[8,4,6656]{2,1,0:T(4,128)(2,1)S(1)}, f32[8,32]{1,0:T(8,128)S(1)}, bf16[6144,512]{1,0:T(8,128)(2,1)S(1)}, bf16[6144,512]{1,0:T(8,128)(2,1)S(1)}) custom-call(s32[1]{0:T(128)S(6)} %copy.17.lengths, s32[6]{0:T(128)S(1)} %copy-done.1, s32[2,6]{1,0:T(2,128)S(1)} %bitcast.3, s32[1]{0:T(128)S(6)} %copy.18.accepted, ...), custom_call_target="tpu_custom_call" | custom-call | tf_op jit(solution)/shard_map/pallas_call | solution.py:496
  9.3 19.7 %all_to_all.20.mine = bf16[8,4,6656]{2,1,0:T(4,128)(2,1)S(1)} all-to-all(bf16[8,4,6656]{2,1,0:T(4,128)(2,1)S(1)} %get-tuple-element.15), channel_id=1, replica_groups={{0,2,4,6,8,10,12,14},{1,3,5,7,9,11,13,15},{16,18,20,22,24,26,28,30},{17..., dimensions={0} | all-to-all | bytes 851968 | tf_op jit(solution)/shard_map/all_to_all | solution.py:544
  29.0 0.0 collective-permute-start
  29.0 1.8 %collective-permute-done.other = bf16[8,4,6656]{2,1,0:T(4,128)(2,1)S(1)} collective-permute-done((bf16[8,4,6656]{2,1,0:T(4,128)(2,1)S(1)}, bf16[8,4,6656]{2,1,0:T(4,128)(2,1)S(1)}, u32[]{:S(2)}, u32[]{:S(2)}) %collective-permute-start) | collective-permute-done | bytes 426016 | tf_op jit(solution)/shard_map/ppermute | solution.py:547
  30.8 21.6 %shard_map.159 = (f32[32,6144]{1,0:T(8,128)S(1)}, bf16[32,6144]{1,0:T(8,128)(2,1)S(1)}, bf16[64,384]{1,0:T(8,128)(2,1)S(1)}, f32[64,128]{1,0:T(8,128)S(1)}) custom-call(bf16[8,4,6656]{2,1,0:T(4,128)(2,1)S(1)} %all_to_all.20.mine, bf16[8,4,6656]{2,1,0:T(4,128)(2,1)S(1)} %collective-permute-done.other, bf16[6144,512]{1,0:T(8,128)(2,1)S(1)} %get-tuple-element.16.gate_first, ...), custom_call_target="tpu_custom_call" | custom-call | flops 4831838208 | bytes 75497472 | tf_op jit(solution)/shard_map/pallas_call | solution.py:551
  52.4 0.2 collective-permute-start.1
  52.6 1.6 %collective-permute-done.1.came = bf16[32,6144]{1,0:T(8,128)(2,1)S(1)} collective-permute-done((bf16[32,6144]{1,0:T(8,128)(2,1)S(1)}, bf16[32,6144]{1,0:T(8,128)(2,1)S(1)}, u32[]{:S(2)}, u32[]{:S(2)}) %collective-permute-start.1) | collective-permute-done | bytes 393248 | tf_op jit(solution)/shard_map/ppermute | solution.py:586
  54.2 0.9 shard_map.160
  55.1 12.2 %all_to_all.21.came = bf16[16,8,768]{2,1,0:T(8,128)(2,1)S(1)} all-to-all(bf16[16,8,768]{2,1,0:T(8,128)(2,1)S(1)} %get-tuple-element.22), channel_id=1, replica_groups=mesh['groups'=2,'expert'=16] {'expert'}, dimensions={0} | all-to-all | bytes 393216 | tf_op jit(solution)/shard_map/all_to_all | solution.py:601
  67.4 3.5 %all-to-all-start.1 = ((bf16[8,4,6144]{2,1,0:T(4,128)(2,1)}), bf16[8,4,6144]{2,1,0:T(4,128)(2,1)S(1)}, u32[]{:S(2)}, u32[]{:S(2)}) async-start(bf16[8,4,6144]{2,1,0:T(4,128)(2,1)} %get-tuple-element.21), calls=%async_computation.1 | async-start | bytes 786432 | tf_op jit(solution)/shard_map/all_to_all | solution.py:602
  70.8 4.8 %shard_map.162 = bf16[16,8,768]{2,1,0:T(8,128)(2,1)} custom-call(bf16[16,8,768]{2,1,0:T(8,128)(2,1)S(1)} %all_to_all.21.came, bf16[64,384]{1,0:T(8,128)(2,1)S(1)} %get-tuple-element.23.notes, bf16[768,6144]{1,0:T(8,128)(2,1)} %fc.1), custom_call_target="tpu_custom_call" | custom-call | tf_op jit(solution)/shard_map/pallas_call | solution.py:605
  75.7 6.9 %all-to-all-done.1.came = bf16[8,4,6144]{2,1,0:T(4,128)(2,1)S(1)} async-done(((bf16[8,4,6144]{2,1,0:T(4,128)(2,1)}), bf16[8,4,6144]{2,1,0:T(4,128)(2,1)S(1)}, u32[]{:S(2)}, u32[]{:S(2)}) %all-to-all-start.1) | async-done | bytes 393248 | tf_op jit(solution)/shard_map/all_to_all | solution.py:602
  82.6 3.7 %all-to-all-start.3 = ((bf16[16,8,768]{2,1,0:T(8,128)(2,1)}), bf16[16,8,768]{2,1,0:T(8,128)(2,1)S(1)}, u32[]{:S(2)}, u32[]{:S(2)}) async-start(bf16[16,8,768]{2,1,0:T(8,128)(2,1)} %shard_map.162), calls=%async_computation.3 | async-start | bytes 393216 | tf_op jit(solution)/shard_map/all_to_all | solution.py:617
  86.3 0.9 shard_map.161
  87.2 8.1 %all-to-all-done.3.came = bf16[16,8,768]{2,1,0:T(8,128)(2,1)S(1)} async-done(((bf16[16,8,768]{2,1,0:T(8,128)(2,1)}), bf16[16,8,768]{2,1,0:T(8,128)(2,1)S(1)}, u32[]{:S(2)}, u32[]{:S(2)}) %all-to-all-start.3) | async-done | bytes 196640 | tf_op jit(solution)/shard_map/all_to_all | solution.py:617
  95.3 0.6 shard_map.163
Async XLA Ops:
  1.9 0.7 copy-start
  2.6 0.7 copy-start.1
  29.0 1.8 %collective-permute-start = (bf16[8,4,6656]{2,1,0:T(4,128)(2,1)S(1)}, bf16[8,4,6656]{2,1,0:T(4,128)(2,1)S(1)}, u32[]{:S(2)}, u32[]{:S(2)}) collective-permute-start(bf16[8,4,6656]{2,1,0:T(4,128)(2,1)S(1)} %all_to_all.20.mine), channel_id=1, source_target_pairs={{0,1},{1,0},{2,3},{3,2},{4,5},{5,4},{6,7},{7,6},{8,9},{9,8},{10,11... | collective-permute-start | bytes 1277960 | tf_op jit(solution)/shard_map/ppermute | solution.py:547
  52.4 1.8 %collective-permute-start.1 = (bf16[32,6144]{1,0:T(8,128)(2,1)S(1)}, bf16[32,6144]{1,0:T(8,128)(2,1)S(1)}, u32[]{:S(2)}, u32[]{:S(2)}) collective-permute-start(bf16[32,6144]{1,0:T(8,128)(2,1)S(1)} %get-tuple-element.19), channel_id=1, source_target_pairs={{0,1},{1,0},{2,3},{3,2},{4,5},{5,4},{6,7},{7,6},{8,9},{9,8},{10,11... | collective-permute-start | bytes 1179656 | tf_op jit(solution)/shard_map/ppermute | solution.py:586
  67.4 15.2 %all-to-all-start.1 = ((bf16[8,4,6144]{2,1,0:T(4,128)(2,1)}), bf16[8,4,6144]{2,1,0:T(4,128)(2,1)S(1)}, u32[]{:S(2)}, u32[]{:S(2)}) async-start(bf16[8,4,6144]{2,1,0:T(4,128)(2,1)} %get-tuple-element.21), calls=%async_computation.1 | async-start | bytes 786432 | tf_op jit(solution)/shard_map/all_to_all | solution.py:602
  82.6 12.7 %all-to-all-start.3 = ((bf16[16,8,768]{2,1,0:T(8,128)(2,1)}), bf16[16,8,768]{2,1,0:T(8,128)(2,1)S(1)}, u32[]{:S(2)}, u32[]{:S(2)}) async-start(bf16[16,8,768]{2,1,0:T(8,128)(2,1)} %shard_map.162), calls=%async_computation.3 | async-start | bytes 393216 | tf_op jit(solution)/shard_map/all_to_all | solution.py:617

commit v3 on v2

v3 whole, which is shorter than its diff:
```python
import functools
import jax
import jax.numpy as jnp
from jax import lax
from jax.experimental import pallas as pl
from jax.experimental.pallas import tpu as pltpu
from jax.sharding import PartitionSpec as P

QUERY_HEADS = 48
KEY_VALUE_HEADS = 8
HEAD_SIZE = 128
EXPERTS = 4
TREE_NODES = 6
CAP = 4
ROWS = 8
LANES = 128
EPSILON = 1e-05
HIDDEN = -1e30

F32 = jnp.float32
BF16 = jnp.bfloat16
VMEM = pltpu.VMEM
SMEM = pltpu.SMEM
MIB = 1 << 20


def spec(space):
    return pl.BlockSpec(memory_space=space)


def iota(shape, axis):
    return lax.broadcasted_iota(jnp.int32, shape, axis)


def along(values, shape, axis, fill=-1):
    index = iota(shape, axis)
    out = jnp.full(shape, fill, jnp.int32)
    for at, value in enumerate(values):
        out = jnp.where(index == at, value, out)
    return out


def attend(
    lengths,
    accepted,
    parents_far,
    routes_far,
    queries_far,
    tree_far,
    cache,
    residual_far,
    gain_far,
    router_far,
    embed_far,
    gate,
    up,
    hidden_out,
    send_0,
    send_1,
    send_2,
    send_3,
    placing_out,
    gate_first,
    up_first,
    parents,
    routes,
    queries,
    tree_key_value,
    keys,
    values,
    residual,
    gain,
    router,
    embed,
    tree,
    padded,
    hidden,
    payload,
    sems,
):
    width = queries.shape[1]
    per_expert = placing_out.shape[1] // (CAP * EXPERTS)
    draft_cols = payload.shape[2] - width - LANES
    shared = QUERY_HEADS // KEY_VALUE_HEADS
    first = gate_first.shape[1]
    moves = [
        (parents_far, parents),
        (routes_far, routes),
        (queries_far, queries),
        (tree_far, tree_key_value),
        (cache.at[0, 0], keys),
        (cache.at[0, 1], values),
        (residual_far, residual),
        (gain_far, gain),
        (router_far, router),
        (embed_far, embed),
        (gate.at[:, pl.ds(0, first)], gate_first),
        (up.at[:, pl.ds(0, first)], up_first),
    ]
    copies = [
        pltpu.make_async_copy(source, target, sems.at[i])
        for i, (source, target) in enumerate(moves)
    ]
    for copy in copies:
        copy.start()
    for copy in copies[:2]:
        copy.wait()

    bits = []
    for t in range(TREE_NODES):
        above = jnp.int32(0)
        for j in range(t):
            above = jnp.where(parents[t] == j, bits[j], above)
        bits.append(above | (1 << t))
    counts = [jnp.int32(0)] * EXPERTS
    slots = [[], []]
    for t in range(TREE_NODES):
        for k in range(2):
            slot = jnp.int32(0)
            for e in range(EXPERTS):
                slot = jnp.where(routes[k, t] == e, e * CAP + counts[e], slot)
            slots[k].append(slot)
        for e in range(EXPERTS):
            named = jnp.logical_or(routes[0, t] == e, routes[1, t] == e)
            counts[e] = counts[e] + named.astype(jnp.int32)

    tree[...] = jnp.zeros(tree.shape, F32)
    copies[2].wait()
    copies[3].wait()
    for t in range(TREE_NODES):
        pair = tree_key_value[t].astype(F32)
        tree[0, t : t + 1, :] = pair[0:1]
        tree[1, t : t + 1, :] = pair[1:2]
    padded[...] = jnp.zeros(padded.shape, F32)
    padded[0:TREE_NODES, :] = queries[...].astype(F32)

    slots_total = keys.shape[0]
    visible = iota((shared * ROWS, slots_total), 1) < lengths[0]
    row = iota((shared * ROWS, ROWS), 0) & (ROWS - 1)
    row_bits = jnp.ones((shared * ROWS, ROWS), jnp.int32)
    for t in range(TREE_NODES):
        row_bits = jnp.where(row == t, bits[t], row_bits)
    related = ((row_bits >> iota((shared * ROWS, ROWS), 1)) & 1) == 1
    scale = HEAD_SIZE ** (-0.5)
    contract_last = (((1,), (1,)), ((), ()))
    for copy in copies[4:10]:
        copy.wait()
    hidden[...] = jnp.zeros(hidden.shape, F32)
    hidden[0:TREE_NODES, :] = residual[...].astype(F32)
    for g in range(KEY_VALUE_HEADS):
        head = slice(g * HEAD_SIZE, (g + 1) * HEAD_SIZE)
        block = jnp.concatenate(
            [
                padded[:, (g * shared + i) * HEAD_SIZE : (g * shared + i + 1) * HEAD_SIZE]
                for i in range(shared)
            ],
            axis=0,
        ).astype(BF16)
        cache_scores = (
            lax.dot_general(block, keys[:, head], contract_last, preferred_element_type=F32)
            * scale
        )
        tree_scores = (
            lax.dot_general(
                block, tree[0, :, head].astype(BF16), contract_last, preferred_element_type=F32
            )
            * scale
        )
        cache_scores = jnp.where(visible, cache_scores, HIDDEN)
        tree_scores = jnp.where(related, tree_scores, HIDDEN)
        peak = jnp.maximum(
            jnp.max(cache_scores, axis=1, keepdims=True),
            jnp.max(tree_scores, axis=1, keepdims=True),
        )
        cache_exp = jnp.exp(cache_scores - peak)
        tree_exp = jnp.exp(tree_scores - peak)
        total = jnp.sum(cache_exp, axis=1, keepdims=True) + jnp.sum(
            tree_exp, axis=1, keepdims=True
        )
        share = 1.0 / total
        context = jnp.dot(
            (cache_exp * share).astype(BF16), values[:, head], preferred_element_type=F32
        ) + jnp.dot(
            (tree_exp * share).astype(BF16),
            tree[1, :, head].astype(BF16),
            preferred_element_type=F32,
        )
        for i in range(shared):
            columns = slice((g * shared + i) * HEAD_SIZE, (g * shared + i + 1) * HEAD_SIZE)
            hidden[:, columns] = hidden[:, columns] + context[i * ROWS : (i + 1) * ROWS]

    state = hidden[...]
    hidden_out[...] = state
    mean = jnp.sum(state * state, axis=1, keepdims=True) * (1.0 / width)
    gains = gain[...].astype(F32)
    shrink = lax.rsqrt(mean + EPSILON)
    normed = jnp.concatenate(
        [
            state[:, i * LANES : (i + 1) * LANES] * shrink * gains[i : i + 1]
            for i in range(width // LANES)
        ],
        axis=1,
    ).astype(BF16)
    logits = lax.dot_general(normed, router[...], contract_last, preferred_element_type=F32)
    expert = iota((ROWS, EXPERTS), 1)
    route = [
        along([routes[k, t] for t in range(TREE_NODES)], (ROWS, EXPERTS), 0) for k in range(2)
    ]
    picked_logit = [
        jnp.sum(jnp.where(expert == route[k], logits, 0.0), axis=1, keepdims=True)
        for k in range(2)
    ]
    first = jax.nn.sigmoid(picked_logit[0] - picked_logit[1])
    lane = iota((ROWS, LANES), 1)
    is_accepted = (iota((ROWS, LANES), 0) == accepted[0]).astype(F32)
    extras = []
    for weight in (first, 1.0 - first):
        high = weight.astype(BF16).astype(F32)
        extras.append(
            jnp.where(
                lane == 0,
                high,
                jnp.where(lane == 1, weight - high, jnp.where(lane == 2, is_accepted, 0.0)),
            ).astype(BF16)
        )
    place_row = iota((EXPERTS * ROWS, ROWS), 0)
    target = (place_row // ROWS) * CAP + (place_row & (ROWS - 1))
    target = jnp.where((place_row & (ROWS - 1)) < CAP, target, -2)
    hits = [
        (target == along(slots[k], (EXPERTS * ROWS, ROWS), 1)).astype(F32).astype(BF16)
        for k in range(2)
    ]
    packed = jnp.dot(hits[0] + hits[1], normed, preferred_element_type=F32)
    extra = jnp.dot(hits[0], extras[0], preferred_element_type=F32) + jnp.dot(
        hits[1], extras[1], preferred_element_type=F32
    )
    for e in range(EXPERTS):
        rows = packed[e * ROWS : e * ROWS + CAP].astype(BF16)
        last = extra[e * ROWS : e * ROWS + CAP].astype(BF16)
        payload[e, :, 0:width] = rows
        payload[e, :, width + draft_cols :] = last
    chosen = jnp.sum(
        jnp.where(iota((ROWS, width), 0) == accepted[0], state, 0.0), axis=0, keepdims=True
    )
    rest = embed[...].astype(F32)
    for e in range(EXPERTS):
        for i in range(CAP):
            at = (e * CAP + i) * draft_cols
            source = chosen if at < width else rest
            at = at % width
            payload[e, i : i + 1, width : width + draft_cols] = source[
                :, at : at + draft_cols
            ].astype(BF16)
    mine = lax.axis_index("expert") // (2 * per_expert)
    for shift, target in enumerate((send_0, send_1, send_2, send_3)):
        target[...] = payload[lax.rem(mine + shift, EXPERTS)]
    lane_slot = iota(placing_out.shape, 1)
    lane_slot = (lane_slot // (CAP * per_expert)) * CAP + lane_slot % CAP
    placing_out[...] = jnp.logical_or(
        lane_slot == along(slots[0], placing_out.shape, 0),
        lane_slot == along(slots[1], placing_out.shape, 0),
    ).astype(F32)
    for copy in copies[10:]:
        copy.wait()


def fetch(first, after, gate, up, gate_next, up_next, sems):
    del after
    columns = pl.ds(first, gate_next.shape[1])
    copies = [
        pltpu.make_async_copy(gate.at[:, columns], gate_next, sems.at[0]),
        pltpu.make_async_copy(up.at[:, columns], up_next, sems.at[1]),
    ]
    for copy in copies:
        copy.start()
    for copy in copies:
        copy.wait()


def join(*refs):
    for i, ref in enumerate(refs[:-1]):
        refs[-1][i] = ref[...]


def experts(width, sources, held, *refs):
    pieces, refs = refs[:sources], refs[sources:]
    ready, refs = refs[: 2 * held], refs[2 * held :]
    stream(width, pieces, ready, *refs)


def stream(
    width,
    pieces,
    ready,
    gate,
    up,
    down,
    keep,
    send,
    notes,
    weights,
    rows,
    acts,
    units,
    sems,
):
    whole_width = pieces[0].shape[2]
    half = keep.shape[0]
    count, depth, chunk = units.shape
    first = sum(block.shape[1] for block in ready[::2])
    parts = width // depth
    queue = []
    spans = [(at, min(chunk, depth - at)) for at in range(first, depth, chunk)]
    for at, span in spans:
        for source in (gate, up):
            for p in range(parts):
                queue.append((source.at[pl.ds(p * depth, depth), pl.ds(at, span)], span))
    for at in range(0, width, chunk):
        queue.append((down.at[:, pl.ds(at, chunk)], chunk))
    copies = [
        pltpu.make_async_copy(
            source, units.at[i % count, :, pl.ds(0, span)], sems.at[i % count]
        )
        for i, (source, span) in enumerate(queue)
    ]
    for copy in copies[:count]:
        copy.start()
    taken = 0

    def product(left):
        nonlocal taken
        copies[taken].wait()
        span = queue[taken][1]
        result = jnp.dot(
            left, units[taken % count, :, 0:span], preferred_element_type=F32
        )
        if taken + count < len(copies):
            copies[taken + count].start()
        taken += 1
        return result

    for k, source in enumerate(pieces):
        at = slice(k * EXPERTS * CAP, (k + 1) * EXPERTS * CAP)
        full = jnp.concatenate([source[z].astype(F32) for z in range(EXPERTS)], axis=0)
        rows[at, :] = full[:, 0:width].astype(BF16)
        notes[at, :] = full[:, width : whole_width - LANES].astype(BF16)
        weights[at, :] = full[:, whole_width - LANES :]
    if rows.shape[0] > 2 * half:
        rows[2 * half :, :] = jnp.zeros((rows.shape[0] - 2 * half, width), BF16)

    def activate(gate_val, up_val, at):
        acts[:, at : at + gate_val.shape[1]] = (
            gate_val / (1.0 + jnp.exp(-gate_val)) * up_val
        ).astype(BF16)

    base = 0
    for gate_block, up_block in zip(ready[::2], ready[1::2]):
        activate(
            jnp.dot(rows[...], gate_block[...], preferred_element_type=F32),
            jnp.dot(rows[...], up_block[...], preferred_element_type=F32),
            base,
        )
        base += gate_block.shape[1]
    for at, _ in spans:
        gate_val, up_val = [
            sum(product(rows[:, p * depth : (p + 1) * depth]) for p in range(parts))
            for _ in range(2)
        ]
        activate(gate_val, up_val, at)
    mix = weights[:, 0:1] + weights[:, 1:2]
    for at in range(0, width, chunk):
        result = product(acts[...])[: 2 * half] * mix
        keep[:, at : at + chunk] = result[:half]
        send[:, at : at + chunk] = result[half:].astype(BF16)


def place_of(masks, member, shape, axis):
    block = iota(shape, axis) // CAP
    chip = jnp.zeros(shape, jnp.int32)
    for k, mask in enumerate(masks[: len(masks) // 2]):
        chip = jnp.where(block // EXPERTS == k, (member ^ mask) >> 1, chip)
    plane = (lax.axis_index("expert") // len(masks) + EXPERTS - block % EXPERTS) % EXPERTS
    return plane * (len(masks) // 2) + chip


def combine(masks, keep, came, flags, returned, chosen_out):
    chips = returned.shape[0]
    half, width = keep.shape
    group = len(masks)
    member = lax.axis_index("expert") % group
    total = keep[...] + came[...].astype(F32)
    for k, mask in enumerate(masks[: group // 2]):
        for z in range(EXPERTS):
            at = (k * EXPERTS + z) * CAP
            plane = lax.rem(lax.axis_index("expert") // group + EXPERTS - z, EXPERTS)
            chip = plane * (group // 2) + ((member ^ mask) >> 1)
            returned[chip, :, 0:width] = total[at : at + CAP].astype(BF16)
    rounded = total.astype(BF16)
    turns = chips // CAP
    place = place_of(masks, member, (half, ROWS), 0)
    wanted = iota((half, ROWS), 1) * turns
    span = (returned.shape[2] - width) // turns
    for r in range(turns):
        select = jnp.where(place == wanted + r, flags[0:half, 2:3], 0.0).astype(BF16)
        chosen = lax.dot_general(
            select, rounded, (((0,), (0,)), ((), ())), preferred_element_type=F32
        )[:CAP].astype(BF16)
        if span % LANES:
            chosen_out[r] = chosen
            continue
        columns = slice(width + r * span, width + (r + 1) * span)
        for q in range(chips):
            if q * span < width:
                returned[q, :, columns] = chosen[:, q * span : (q + 1) * span]
            else:
                returned[q, :, columns] = jnp.zeros((CAP, span), BF16)


def gather(width, came, out):
    chips = came.shape[0]
    turns = chips // CAP
    span = out.shape[1]
    total = came[0, :, width:].astype(F32)
    for q in range(1, chips):
        total = total + came[q, :, width:].astype(F32)
    for r in range(turns):
        out[r * CAP : (r + 1) * CAP, :] = total[:, r * span : (r + 1) * span]


def draft_fetch(masks, notes, fc, fc_out, early, sems):
    copy = pltpu.make_async_copy(fc.at[:, pl.ds(0, fc_out.shape[1])], fc_out, sems.at[0])
    copy.start()
    chips = early.shape[0] // 2
    half = notes.shape[0] // 2
    group = len(masks)
    me = lax.axis_index("expert")
    member, core = me % group, me % 2
    place = place_of(masks, member, (chips, half), 1)
    row = iota((chips, half), 0)
    wanted = (row % CAP) * (chips // CAP) + row // CAP
    select = jnp.logical_and(place == wanted, iota((chips, half), 1) % CAP == member)
    select = select.astype(F32).astype(BF16)
    same, other = [
        jnp.dot(
            select, notes[side * half : (side + 1) * half, :], preferred_element_type=F32
        )
        for side in range(2)
    ]
    early[0:chips, :] = jnp.where(core == 0, same, other)
    early[chips:, :] = jnp.where(core == 0, other, same)
    copy.wait()


def project(mine, other, early, fc_first, fc, out, rest, spread, sems):
    chips = mine.shape[0]
    devices, columns = early.shape
    pieces, step = out.shape[1:]
    ready = fc_first.shape[1] // step
    copies = [
        pltpu.make_async_copy(
            fc.at[:, pl.ds(i * step, step)], rest.at[i - ready], sems.at[i - ready]
        )
        for i in range(ready, pieces)
    ]
    for copy in copies:
        copy.start()
    core = lax.axis_index("expert") % 2
    sums = []
    for pair in ((mine, other), (other, mine)):
        total = jnp.where(core == 0, pair[0][...], pair[1][...])
        sums.append(jnp.where(core == 0, total[:, :columns], total[:, columns:]))
    inputs = (jnp.concatenate(sums, axis=0) + early[...]).astype(BF16)
    for i in range(pieces):
        if i < ready:
            block = fc_first[:, i * step : (i + 1) * step]
        else:
            copies[i - ready].wait()
            block = rest[i - ready]
        result = jnp.dot(inputs, block, preferred_element_type=F32)
        for k in range(step // LANES):
            spread[k, pl.ds(i, devices, stride=pieces), :] = result[
                :, k * LANES : (k + 1) * LANES
            ]
    turns = chips // CAP
    for c in range(2):
        for r in range(turns):
            for i in range(CAP):
                at = (c * chips + r * CAP + i) * pieces
                for k in range(step // LANES):
                    out[2 * (i * turns + r) + c, :, k * LANES : (k + 1) * LANES] = spread[
                        k, at : at + pieces, :
                    ].astype(BF16)


def finish(came, out):
    total = came[0].astype(F32)
    for d in range(1, came.shape[0]):
        total = total + came[d].astype(F32)
    step = total.shape[1]
    for i in range(total.shape[0]):
        out[:, i * step : (i + 1) * step] = total[i : i + 1].astype(BF16)


def settle(hidden, placing, came, out):
    chips = came.shape[0]
    width = out.shape[1]
    rows = jnp.concatenate(
        [came[q, :, 0:width].astype(F32) for q in range(chips)], axis=0
    ).astype(BF16)
    total = hidden[...] + jnp.dot(
        placing[...].astype(BF16), rows, preferred_element_type=F32
    )
    out[...] = total[: out.shape[0]].astype(BF16)


def far(array):
    return pltpu.with_memory_space_constraint(array, pltpu.HBM)


def near(array):
    return pltpu.with_memory_space_constraint(array, VMEM)


def early_of(notes, masks, devices, draft_rows):
    group, chips = len(masks), devices // 2
    member = lax.axis_index("expert") % group
    columns = notes.astype(F32).reshape(group, EXPERTS, group, draft_rows)
    columns = lax.dynamic_index_in_dim(columns, member, 2, keepdims=False)
    order = jnp.arange(devices)
    core, rest = order // chips, order % chips
    device = 2 * ((rest % CAP) * (chips // CAP) + rest // CAP) + core
    piece = jnp.zeros((group,), jnp.int32).at[jnp.array(masks)].set(jnp.arange(group))
    shift = (lax.axis_index("expert") // group - device // group) % EXPERTS
    return columns[piece[member ^ (device % group)], shift]


def params(mib):
    return pltpu.CompilerParams(vmem_limit_bytes=mib * MIB)


def per_device(
    queries,
    tree_key_value,
    key_value_cache,
    lengths,
    parents,
    residual,
    ffn_gain,
    router,
    routes,
    gate_weight,
    up_weight,
    down_weight,
    accepted,
    next_embed,
    draft_fc,
):
    devices = lax.axis_size("expert")
    chips = devices // 2
    group = devices // EXPERTS
    tokens, width = queries.shape
    assert lengths.shape[0] == 1 and tokens == TREE_NODES
    cache_slots, key_width = key_value_cache.shape[2:]
    hidden_units = gate_weight.shape[1]
    draft_rows = draft_fc.shape[0]
    ext = group * draft_rows // CAP
    total_width = width + ext + LANES
    same_core = [[2 * q + c for q in range(chips)] for c in range(2)]
    masks = [0]
    bits = [1 << i for i in range(group.bit_length() - 1)]
    for bit in reversed(bits):
        masks = masks + [mask | bit for mask in masks]

    def swap(array, bit):
        return lax.ppermute(array, "expert", [(d, d ^ bit) for d in range(devices)])

    first = 512 if hidden_units > 1024 else hidden_units // 2
    more = (256, 512) if hidden_units > 1024 else ()
    chunk = min(512, first)
    hidden, *parcels, placing, gate_first, up_first = pl.pallas_call(
        attend,
        out_shape=(
            jax.ShapeDtypeStruct((ROWS, width), F32),
            *[jax.ShapeDtypeStruct((CAP, total_width), BF16)] * EXPERTS,
            jax.ShapeDtypeStruct((ROWS, chips * CAP), F32),
            VMEM((width, first), BF16),
            VMEM((width, first), BF16),
        ),
        in_specs=[spec(SMEM)] * 2 + [spec(pl.ANY)] * 11,
        out_specs=(spec(VMEM),) * (4 + EXPERTS),
        scratch_shapes=[
            SMEM(parents.shape, jnp.int32),
            SMEM(routes.shape[::-1], jnp.int32),
            VMEM(queries.shape, BF16),
            VMEM(tree_key_value.shape, BF16),
            VMEM((cache_slots, key_width), BF16),
            VMEM((cache_slots, key_width), BF16),
            VMEM(residual.shape, BF16),
            VMEM((width // LANES, LANES), BF16),
            VMEM((EXPERTS, width), BF16),
            VMEM(next_embed.shape, BF16),
            VMEM((2, ROWS, key_width), F32),
            VMEM((ROWS, width), F32),
            VMEM((ROWS, width), F32),
            VMEM((EXPERTS, CAP, total_width), BF16),
            pltpu.SemaphoreType.DMA((12,)),
        ],
        compiler_params=params(12),
    )(
        lengths,
        accepted,
        far(parents),
        far(routes.T),
        far(queries),
        far(tree_key_value),
        far(key_value_cache),
        far(residual),
        far(ffn_gain.reshape(width // LANES, LANES)),
        far(router.T),
        far(next_embed),
        far(gate_weight),
        far(up_weight),
    )
    ready = [gate_first, up_first]

    def fetch_more(after, ready, more):
        at = sum(block.shape[1] for block in ready[::2])
        return ready + list(pl.pallas_call(
            functools.partial(fetch, at),
            out_shape=(VMEM((width, more), BF16), VMEM((width, more), BF16)),
            in_specs=[spec(pl.ANY)] * 3,
            out_specs=(spec(VMEM),) * 2,
            scratch_shapes=[pltpu.SemaphoreType.DMA((2,))],
            compiler_params=params(1),
            cost_estimate=pl.CostEstimate(
                flops=0, bytes_accessed=4 * width * more * 2, transcendentals=0
            ),
        )(after, far(gate_weight), far(up_weight)))

    for shift in range(1, EXPERTS):
        ring = [(d, (d + shift * group) % devices) for d in range(devices)]
        parcels[shift] = lax.ppermute(parcels[shift], "expert", ring)
    if more:
        ready = fetch_more(placing, ready, more[0])
        ready[-1], *parcels[1:] = lax.optimization_barrier((ready[-1], *parcels[1:]))
    pieces = [
        pl.pallas_call(
            join,
            out_shape=jax.ShapeDtypeStruct((EXPERTS, CAP, total_width), BF16),
            in_specs=[spec(VMEM)] * EXPERTS,
            out_specs=spec(VMEM),
            compiler_params=params(2),
        )(*parcels)
    ]
    for bit in reversed(bits[1:]):
        pieces = pieces + [swap(piece, bit) for piece in pieces]
    if more:
        ready = fetch_more(pieces[0], ready, more[1])
        ready[-1], *pieces[1:] = lax.optimization_barrier((ready[-1], *pieces[1:]))
    pieces = pieces + [swap(piece, 1) for piece in pieces]

    units = 8
    rows = 2 * chips * CAP
    padded_rows = -(-rows // 128) * 128
    keep, send, notes, weights = pl.pallas_call(
        functools.partial(experts, width, len(pieces), len(ready) // 2),
        out_shape=(
            VMEM((chips * CAP, width), F32),
            VMEM((chips * CAP, width), BF16),
            VMEM((rows, ext), BF16),
            VMEM((rows, LANES), F32),
        ),
        in_specs=[spec(VMEM)] * (len(pieces) + len(ready)) + [spec(pl.ANY)] * 3,
        out_specs=(spec(VMEM),) * 4,
        scratch_shapes=[
            VMEM((padded_rows, width), BF16),
            VMEM((padded_rows, hidden_units), BF16),
            VMEM((units, hidden_units, chunk), BF16),
            pltpu.SemaphoreType.DMA((units,)),
        ],
        compiler_params=params(21),
        cost_estimate=pl.CostEstimate(
            flops=2 * rows * width * hidden_units * 3,
            bytes_accessed=3 * down_weight.size * 2,
            transcendentals=0,
        ),
    )(
        *[near(piece) for piece in pieces],
        *[near(block) for block in ready],
        far(gate_weight),
        far(up_weight),
        far(down_weight),
    )
    came = swap(send, 1)
    fc_ready = width // 2
    fc_first, early = pl.pallas_call(
        functools.partial(draft_fetch, masks),
        out_shape=(
            VMEM((draft_rows, fc_ready), BF16),
            VMEM((devices, ext), F32),
        ),
        in_specs=[spec(VMEM), spec(pl.ANY)],
        out_specs=(spec(VMEM),) * 2,
        scratch_shapes=[pltpu.SemaphoreType.DMA((1,))],
        compiler_params=params(4),
        cost_estimate=pl.CostEstimate(
            flops=0, bytes_accessed=2 * draft_rows * fc_ready * 2, transcendentals=0
        ),
    )(near(notes), far(draft_fc))
    came, early = lax.optimization_barrier((came, early))
    span = 2 * draft_rows
    turns = chips // CAP
    partial, chosen = pl.pallas_call(
        functools.partial(combine, masks),
        out_shape=(
            jax.ShapeDtypeStruct((chips, CAP, width + turns * span), BF16),
            jax.ShapeDtypeStruct((turns, CAP, width if span % LANES else LANES), BF16),
        ),
        in_specs=[spec(VMEM)] * 3,
        out_specs=(spec(VMEM),) * 2,
        compiler_params=params(16),
    )(near(keep), came, near(weights))
    if span % LANES:
        chosen = chosen.reshape(turns, CAP, chips // 2, span).transpose(2, 1, 0, 3)
        chosen = chosen.reshape(chips // 2, CAP, turns * span)
        chosen = jnp.concatenate([chosen, jnp.zeros_like(chosen)], axis=0)
        partial = lax.dynamic_update_slice(partial, chosen, (0, 0, width))
    returned = lax.all_to_all(
        partial, "expert", 0, 0, tiled=True, axis_index_groups=same_core
    )
    if span % LANES:
        mine = jnp.sum(returned[:, :, width:].astype(F32), axis=0)
        mine = mine.reshape(CAP, turns, span).transpose(1, 0, 2).reshape(chips, span)
        early = early_of(notes, masks, devices, draft_rows)
    else:
        mine = pl.pallas_call(
            functools.partial(gather, width),
            out_shape=VMEM((chips, span), F32),
            in_specs=[spec(VMEM)],
            out_specs=spec(VMEM),
            compiler_params=params(4),
        )(returned)
    other = swap(mine, 1)
    sums = pl.pallas_call(
        project,
        out_shape=jax.ShapeDtypeStruct((devices, ROWS, width // ROWS), BF16),
        in_specs=[spec(VMEM)] * 4 + [spec(pl.ANY)],
        out_specs=spec(VMEM),
        scratch_shapes=[
            VMEM((ROWS - ROWS * fc_ready // width, draft_rows, width // ROWS), BF16),
            VMEM((width // ROWS // LANES, devices * ROWS, LANES), F32),
            pltpu.SemaphoreType.DMA((ROWS - ROWS * fc_ready // width,)),
        ],
        compiler_params=params(24),
    )(near(mine), other, near(early), near(fc_first), far(draft_fc))
    sums_came = lax.all_to_all(sums, "expert", 0, 0, tiled=True)
    layer_out = pl.pallas_call(
        settle,
        out_shape=jax.ShapeDtypeStruct((tokens, width), BF16),
        in_specs=[spec(VMEM)] * 3,
        out_specs=spec(VMEM),
        compiler_params=params(16),
    )(hidden, placing, returned)
    draft_out = pl.pallas_call(
        finish,
        out_shape=jax.ShapeDtypeStruct((1, width), BF16),
        in_specs=[spec(VMEM)],
        out_specs=spec(VMEM),
        compiler_params=params(8),
    )(sums_came)
    return (layer_out, draft_out)


def solution(mesh):
    return jax.shard_map(
        per_device,
        mesh=mesh,
        in_specs=(
            P(("groups", "expert"), None),
            P(("groups", "expert"), None, None),
            P(("groups", "expert"), None, None, None),
            P(("groups", "expert")),
            P(("groups", "expert")),
            P(("groups", "expert"), None),
            P(),
            P(),
            P(("groups", "expert"), None),
            P(None, "expert"),
            P(None, "expert"),
            P("expert", None),
            P(("groups", "expert")),
            P(("groups", "expert"), None),
            P("expert", None),
        ),
        out_specs=(P(("groups", "expert"), None), P(("groups", "expert"), None)),
        check_vma=False,
    )
```

time: 96.4 us -> 88 us (0.913)
  blocking collectives: 32 us -> 21.3 us
  waiting for transfers between devices: 18.4 us -> 10.7 us
  starting transfers between devices: 7.38 us -> 13.1 us
  Pallas kernels: 34.9 us -> 40.5 us
  local copies, waits for them, and re-layouts: 1.33 us -> 0 us
    all_to_all x2 -> x1, blocking collectives: 32 us -> 21.3 us  [per_device(): lax.all_to_all(partial, 'expert', 0, 0, tiled=True, axis_index_groups=sam...]
    ppermute x2 -> x8, starting transfers between devices: 0.21 us -> 9.57 us  [the longest x3 7.01 us: per_device(): parcels[shift] = lax.ppermute(parcels[shift], 'expert', ring)]
    all_to_all x1 -> x0, waiting for transfers between devices: 6.93 us -> none  [per_device(): lax.all_to_all(partial, 'expert', 0, 0, tiled=True, axis_index_groups=sam...]
    pallas_call x3 -> x8, Pallas kernels: 28.6 us -> 35 us  [the longest x1 18.8 us: per_device(): pl.pallas_call(functools.partial(experts, width, len(pieces), len(ready)...]
    all_to_all x1 -> x0, starting transfers between devices: 3.45 us -> none  [per_device(): lax.all_to_all(partial, 'expert', 0, 0, tiled=True, axis_index_groups=sam...]
    unnamed x4 -> x0, local copies, waits for them, and re-layouts: 1.33 us -> none
    ppermute x2 -> x8, waiting for transfers between devices: 3.35 us -> 2.63 us  [the longest x5 2.5 us: swap(): return lax.ppermute(array, 'expert', [(d, d ^ bit) for d in range(devices)])]
  transfers between devices with their start and end apart: 4 -> 9, of which waited for: 4 -> 5; matrix products, arithmetic and copies ran while one was open for 0% -> 0% of each run, Pallas kernels for 6% -> 12%
where the time goes in v3:
time: 88 us; the launch traced here: 87.7 us
  Pallas kernels  40.5 us (46%)
  blocking collectives  21.3 us (24%)
  starting transfers between devices  13.1 us (15%)
  waiting for transfers between devices  10.7 us (12%)
  between operations  2.03 us (2%)
    all_to_all x1, blocking collectives, per_device(): lax.all_to_all(partial, 'expert', 0, 0, tiled=True, axis_index_groups=sam...  21.3 us
    pallas_call x1, Pallas kernels, per_device(): pl.pallas_call(functools.partial(experts, width, len(pieces), len(ready)...  18.8 us
    all_to_all x1, waiting for transfers between devices, per_device(): sums_came = lax.all_to_all(sums, 'expert', 0, 0, tiled=True)  8.1 us
    pallas_call x2, Pallas kernels, fetch_more(): pl.pallas_call(functools.partial(fetch, at), out_shape=(VMEM((width, more...  7.51 us
    ppermute x3, starting transfers between devices, per_device(): parcels[shift] = lax.ppermute(parcels[shift], 'expert', ring)  7.01 us
    pallas_call x1, Pallas kernels, per_device(): pl.pallas_call(attend, out_shape=(jax.ShapeDtypeStruct((ROWS, width), F32...  5.49 us
    pallas_call x1, Pallas kernels, per_device(): pl.pallas_call(project, out_shape=jax.ShapeDtypeStruct((devices, ROWS, wi...  3.99 us
    all_to_all x1, starting transfers between devices, per_device(): sums_came = lax.all_to_all(sums, 'expert', 0, 0, tiled=True)  3.53 us
  transfers between devices with their start and end apart: 9, of which 5 were waited for; matrix products, arithmetic and copies ran while one was open for 0% of the time, Pallas kernels for 12%

profile of v3, /device:TPU:0, one launch (start us, length us, event | category | flops | bytes accessed | tf_op | source)
XLA Modules:
  0.0 87.7 jit_solution(14683050988417581485)
XLA Ops:
  1.9 5.5 %shard_map.158 = (f32[8,6144]{1,0:T(8,128)S(1)}, bf16[4,7040]{1,0:T(4,128)(2,1)S(1)}, bf16[4,7040]{1,0:T(4,128)(2,1)S(1)}, bf16[4,7040]{1,0:T(4,128)(2,1)S(1)}, ...) custom-call(s32[1]{0:T(128)S(6)} %copy.17.lengths, ...), custom_call_target="tpu_custom_call" | custom-call | tf_op jit(solution)/shard_map/pallas_call | solution.py:580
  7.4 3.1 %collective-permute-start = (bf16[4,7040]{1,0:T(4,128)(2,1)S(1)}, bf16[4,7040]{1,0:T(4,128)(2,1)S(1)}, u32[]{:S(2)}, u32[]{:S(2)}) collective-permute-start(bf16[4,7040]{1,0:T(4,128)(2,1)S(1)} %get-tuple-element.33), channel_id=1, source_target_pairs={{0,4},{1,5},{2,6},{3,7},{4,8},{5,9},{6,10},{7,11},{8,12},{9,13},{1... | collective-permute-start | bytes 168968 | tf_op jit(solution)/shard_map/ppermute | solution.py:642
  10.5 2.6 %collective-permute-start.1 = (bf16[4,7040]{1,0:T(4,128)(2,1)S(1)}, bf16[4,7040]{1,0:T(4,128)(2,1)S(1)}, u32[]{:S(2)}, u32[]{:S(2)}) collective-permute-start(bf16[4,7040]{1,0:T(4,128)(2,1)S(1)} %get-tuple-element.34), channel_id=1, source_target_pairs={{0,8},{1,9},{2,10},{3,11},{4,12},{5,13},{6,14},{7,15},{8,0},{9,1},... | collective-permute-start | bytes 168968 | tf_op jit(solution)/shard_map/ppermute | solution.py:642
  13.1 1.3 %collective-permute-start.2 = (bf16[4,7040]{1,0:T(4,128)(2,1)S(1)}, bf16[4,7040]{1,0:T(4,128)(2,1)S(1)}, u32[]{:S(2)}, u32[]{:S(2)}) collective-permute-start(bf16[4,7040]{1,0:T(4,128)(2,1)S(1)} %get-tuple-element.35), channel_id=1, source_target_pairs={{0,12},{1,13},{2,14},{3,15},{4,0},{5,1},{6,2},{7,3},{8,4},{9,5},{1... | collective-permute-start | bytes 168968 | tf_op jit(solution)/shard_map/ppermute | solution.py:642
  14.4 2.9 %shard_map.159 = (bf16[6144,256]{1,0:T(8,128)(2,1)S(1)}, bf16[6144,256]{1,0:T(8,128)(2,1)S(1)}) custom-call(f32[8,32]{1,0:T(8,128)S(1)} %get-tuple-element.30.after.placing, bf16[6144,2048]{1,0:T(8,128)(2,1)} %refs_10_.1, bf16[6144,2048]{1,0:T(8,128)(2,1)} %refs_11_.1), custom_call_target="tpu_custom_call" | custom-call | bytes 12582912 | tf_op jit(solution)/shard_map/pallas_call | solution.py:628
  17.3 0.0 collective-permute-done.refs_1_
  17.3 0.0 collective-permute-done.1.refs_2_
  17.3 0.1 collective-permute-done.2.refs_3_
  17.5 1.6 %collective-permute-start.3 = (bf16[4,4,7040]{2,1,0:T(4,128)(2,1)S(1)}, bf16[4,4,7040]{2,1,0:T(4,128)(2,1)S(1)}, u32[]{:S(2)}, u32[]{:S(2)}) collective-permute-start(bf16[4,4,7040]{2,1,0:T(4,128)(2,1)S(1)} %shard_map.160.after.refs_0_), channel_id=1, source_target_pairs={{0,2},{1,3},{2,0},{3,1},{4,6},{5,7},{6,4},{7,5},{8,10},{9,11},{10,... | collective-permute-start | bytes 675848 | tf_op jit(solution)/shard_map/ppermute | solution.py:575
  19.1 0.0 collective-permute-start.4
  19.1 4.6 %shard_map.161 = (bf16[6144,512]{1,0:T(8,128)(2,1)S(1)}, bf16[6144,512]{1,0:T(8,128)(2,1)S(1)}) custom-call(bf16[4,4,7040]{2,1,0:T(4,128)(2,1)S(1)} %shard_map.160.after.refs_0_, bf16[6144,2048]{1,0:T(8,128)(2,1)} %refs_10_.1, bf16[6144,2048]{1,0:T(8,128)(2,1)} %refs_11_.1), custom_call_target="tpu_custom_call" | custom-call | bytes 25165824 | tf_op jit(solution)/shard_map/pallas_call | solution.py:628
  23.8 0.2 collective-permute-done.3.refs_1_
  23.9 0.4 collective-permute-start.5
  24.3 0.0 collective-permute-done.4.refs_2_
  24.3 1.1 %collective-permute-done.5.refs_3_ = bf16[4,4,7040]{2,1,0:T(4,128)(2,1)S(1)} collective-permute-done((bf16[4,4,7040]{2,1,0:T(4,128)(2,1)S(1)}, bf16[4,4,7040]{2,1,0:T(4,128)(2,1)S(1)}, u32[]{:S(2)}, u32[]{:S(2)}) %collective-permute-start.5) | collective-permute-done | bytes 225312 | tf_op jit(solution)/shard_map/ppermute | solution.py:575
  25.5 18.8 %shard_map.162 = (f32[32,6144]{1,0:T(8,128)S(1)}, bf16[32,6144]{1,0:T(8,128)(2,1)S(1)}, bf16[64,768]{1,0:T(8,128)(2,1)S(1)}, f32[64,128]{1,0:T(8,128)S(1)}) custom-call(bf16[4,4,7040]{2,1,0:T(4,128)(2,1)S(1)} %shard_map.160.after.refs_0_, bf16[4,4,7040]{2,1,0:T(4,128)(2,1)S(1)} %collective-permute-done.3.refs_1_, ...), custom_call_target="tpu_custom_call" | custom-call | flops 4831838208 | bytes 75497472 | tf_op jit(solution)/shard_map/pallas_call | solution.py:665
  44.3 0.4 collective-permute-start.6
  44.8 2.4 %shard_map.163 = (bf16[768,3072]{1,0:T(8,128)(2,1)S(1)}, f32[16,768]{1,0:T(8,128)S(1)}) custom-call(bf16[64,768]{1,0:T(8,128)(2,1)S(1)} %get-tuple-element.49.notes, bf16[768,6144]{1,0:T(8,128)(2,1)} %fc.3), custom_call_target="tpu_custom_call" | custom-call | bytes 9437184 | tf_op jit(solution)/shard_map/pallas_call | solution.py:696
  47.1 0.0 collective-permute-done.6.came
  47.1 0.8 shard_map.164
  47.9 21.3 %all_to_all.10.came = bf16[8,4,9216]{2,1,0:T(4,128)(2,1)S(1)} all-to-all(bf16[8,4,9216]{2,1,0:T(4,128)(2,1)S(1)} %get-tuple-element.53), channel_id=1, replica_groups={{0,2,4,6,8,10,12,14},{1,3,5,7,9,11,13,15},{16,18,20,22,24,26,28,30},{17..., dimensions={0} | all-to-all | bytes 1179648 | tf_op jit(solution)/shard_map/all_to_all | solution.py:728
  69.3 0.1 collective-permute-start.7
  69.3 1.2 %collective-permute-done.7.other = f32[8,1536]{1,0:T(8,128)S(1)} collective-permute-done((f32[8,1536]{1,0:T(8,128)S(1)}, f32[8,1536]{1,0:T(8,128)S(1)}, u32[]{:S(2)}, u32[]{:S(2)}) %collective-permute-start.7) | collective-permute-done | bytes 49184 | tf_op jit(solution)/shard_map/ppermute | solution.py:575
  70.6 4.0 %shard_map.167 = bf16[16,8,768]{2,1,0:T(8,128)(2,1)} custom-call(f32[8,1536]{1,0:T(8,128)S(1)} %shard_map.166.mine, f32[8,1536]{1,0:T(8,128)S(1)} %collective-permute-done.7.other, f32[16,768]{1,0:T(8,128)S(1)} %get-tuple-element.54.early, bf16[768,3072]{1,0:T(8,128)(2,1)S(1)} %get-tuple-element.55.fc_first, bf16[768,6144]{1,0:T(8,128)(2,1)} %fc.3), custom_call_target="tpu_custom_call" | custom-call | tf_op jit(solution)/shard_map/pallas_call | solution.py:744
  74.6 3.5 %all-to-all-start.1 = ((bf16[16,8,768]{2,1,0:T(8,128)(2,1)}), bf16[16,8,768]{2,1,0:T(8,128)(2,1)S(1)}, u32[]{:S(2)}, u32[]{:S(2)}) async-start(bf16[16,8,768]{2,1,0:T(8,128)(2,1)} %shard_map.167), calls=%async_computation.1 | async-start | bytes 393216 | tf_op jit(solution)/shard_map/all_to_all | solution.py:756
  78.1 0.9 shard_map.165
  79.0 8.1 %all-to-all-done.1.came = bf16[16,8,768]{2,1,0:T(8,128)(2,1)S(1)} async-done(((bf16[16,8,768]{2,1,0:T(8,128)(2,1)}), bf16[16,8,768]{2,1,0:T(8,128)(2,1)S(1)}, u32[]{:S(2)}, u32[]{:S(2)}) %all-to-all-start.1) | async-done | bytes 196640 | tf_op jit(solution)/shard_map/all_to_all | solution.py:756
  87.1 0.6 shard_map.168
  (2 shorter events, 0.0 us)
Async XLA Ops:
  7.4 9.9 %collective-permute-start = (bf16[4,7040]{1,0:T(4,128)(2,1)S(1)}, bf16[4,7040]{1,0:T(4,128)(2,1)S(1)}, u32[]{:S(2)}, u32[]{:S(2)}) collective-permute-start(bf16[4,7040]{1,0:T(4,128)(2,1)S(1)} %get-tuple-element.33), channel_id=1, source_target_pairs={{0,4},{1,5},{2,6},{3,7},{4,8},{5,9},{6,10},{7,11},{8,12},{9,13},{1... | collective-permute-start | bytes 168968 | tf_op jit(solution)/shard_map/ppermute | solution.py:642
  10.5 6.8 %collective-permute-start.1 = (bf16[4,7040]{1,0:T(4,128)(2,1)S(1)}, bf16[4,7040]{1,0:T(4,128)(2,1)S(1)}, u32[]{:S(2)}, u32[]{:S(2)}) collective-permute-start(bf16[4,7040]{1,0:T(4,128)(2,1)S(1)} %get-tuple-element.34), channel_id=1, source_target_pairs={{0,8},{1,9},{2,10},{3,11},{4,12},{5,13},{6,14},{7,15},{8,0},{9,1},... | collective-permute-start | bytes 168968 | tf_op jit(solution)/shard_map/ppermute | solution.py:642
  13.1 4.4 %collective-permute-start.2 = (bf16[4,7040]{1,0:T(4,128)(2,1)S(1)}, bf16[4,7040]{1,0:T(4,128)(2,1)S(1)}, u32[]{:S(2)}, u32[]{:S(2)}) collective-permute-start(bf16[4,7040]{1,0:T(4,128)(2,1)S(1)} %get-tuple-element.35), channel_id=1, source_target_pairs={{0,12},{1,13},{2,14},{3,15},{4,0},{5,1},{6,2},{7,3},{8,4},{9,5},{1... | collective-permute-start | bytes 168968 | tf_op jit(solution)/shard_map/ppermute | solution.py:642
  17.5 6.5 %collective-permute-start.3 = (bf16[4,4,7040]{2,1,0:T(4,128)(2,1)S(1)}, bf16[4,4,7040]{2,1,0:T(4,128)(2,1)S(1)}, u32[]{:S(2)}, u32[]{:S(2)}) collective-permute-start(bf16[4,4,7040]{2,1,0:T(4,128)(2,1)S(1)} %shard_map.160.after.refs_0_), channel_id=1, source_target_pairs={{0,2},{1,3},{2,0},{3,1},{4,6},{5,7},{6,4},{7,5},{8,10},{9,11},{10,... | collective-permute-start | bytes 675848 | tf_op jit(solution)/shard_map/ppermute | solution.py:575
  19.1 5.2 %collective-permute-start.4 = (bf16[4,4,7040]{2,1,0:T(4,128)(2,1)S(1)}, bf16[4,4,7040]{2,1,0:T(4,128)(2,1)S(1)}, u32[]{:S(2)}, u32[]{:S(2)}) collective-permute-start(bf16[4,4,7040]{2,1,0:T(4,128)(2,1)S(1)} %shard_map.160.after.refs_0_), channel_id=1, source_target_pairs={{0,1},{1,0},{2,3},{3,2},{4,5},{5,4},{6,7},{7,6},{8,9},{9,8},{10,11... | collective-permute-start | bytes 675848 | tf_op jit(solution)/shard_map/ppermute | solution.py:575
  23.9 1.5 %collective-permute-start.5 = (bf16[4,4,7040]{2,1,0:T(4,128)(2,1)S(1)}, bf16[4,4,7040]{2,1,0:T(4,128)(2,1)S(1)}, u32[]{:S(2)}, u32[]{:S(2)}) collective-permute-start(bf16[4,4,7040]{2,1,0:T(4,128)(2,1)S(1)} %collective-permute-done.3.refs_1_), channel_id=1, source_target_pairs={{0,1},{1,0},{2,3},{3,2},{4,5},{5,4},{6,7},{7,6},{8,9},{9,8},{10,11... | collective-permute-start | bytes 675848 | tf_op jit(solution)/shard_map/ppermute | solution.py:575
  44.3 2.8 %collective-permute-start.6 = (bf16[32,6144]{1,0:T(8,128)(2,1)S(1)}, bf16[32,6144]{1,0:T(8,128)(2,1)S(1)}, u32[]{:S(2)}, u32[]{:S(2)}) collective-permute-start(bf16[32,6144]{1,0:T(8,128)(2,1)S(1)} %get-tuple-element.48), channel_id=1, source_target_pairs={{0,1},{1,0},{2,3},{3,2},{4,5},{5,4},{6,7},{7,6},{8,9},{9,8},{10,11... | collective-permute-start | bytes 1179656 | tf_op jit(solution)/shard_map/ppermute | solution.py:575
  69.3 1.3 %collective-permute-start.7 = (f32[8,1536]{1,0:T(8,128)S(1)}, f32[8,1536]{1,0:T(8,128)S(1)}, u32[]{:S(2)}, u32[]{:S(2)}) collective-permute-start(f32[8,1536]{1,0:T(8,128)S(1)} %shard_map.166.mine), channel_id=1, source_target_pairs={{0,1},{1,0},{2,3},{3,2},{4,5},{5,4},{6,7},{7,6},{8,9},{9,8},{10,11... | collective-permute-start | bytes 147464 | tf_op jit(solution)/shard_map/ppermute | solution.py:575
  74.6 12.5 %all-to-all-start.1 = ((bf16[16,8,768]{2,1,0:T(8,128)(2,1)}), bf16[16,8,768]{2,1,0:T(8,128)(2,1)S(1)}, u32[]{:S(2)}, u32[]{:S(2)}) async-start(bf16[16,8,768]{2,1,0:T(8,128)(2,1)} %shard_map.167), calls=%async_computation.1 | async-start | bytes 393216 | tf_op jit(solution)/shard_map/all_to_all | solution.py:756

commit v4 on v3

--- a/solution.py
+++ b/solution.py
@@ -659,7 +659,7 @@
         ready[-1], *pieces[1:] = lax.optimization_barrier((ready[-1], *pieces[1:]))
     pieces = pieces + [swap(piece, 1) for piece in pieces]
 
-    units = 8
+    units = 10
     rows = 2 * chips * CAP
     padded_rows = -(-rows // 128) * 128
     keep, send, notes, weights = pl.pallas_call(
@@ -678,7 +678,7 @@
             VMEM((units, hidden_units, chunk), BF16),
             pltpu.SemaphoreType.DMA((units,)),
         ],
-        compiler_params=params(21),
+        compiler_params=params(25),
         cost_estimate=pl.CostEstimate(
             flops=2 * rows * width * hidden_units * 3,
             bytes_accessed=3 * down_weight.size * 2,

time: 88 us -> 88.1 us (level)
  no operation moved by 1% of the time
where the time goes in v4:
time: 88.1 us; the launch traced here: 87.8 us
  Pallas kernels  40.6 us (46%)
  blocking collectives  21.3 us (24%)
  starting transfers between devices  13.1 us (15%)
  waiting for transfers between devices  10.7 us (12%)
  between operations  2.03 us (2%)
    all_to_all x1, blocking collectives, per_device(): lax.all_to_all(partial, 'expert', 0, 0, tiled=True, axis_index_groups=sam...  21.3 us
    pallas_call x1, Pallas kernels, per_device(): pl.pallas_call(functools.partial(experts, width, len(pieces), len(ready)...  18.9 us
    all_to_all x1, waiting for transfers between devices, per_device(): sums_came = lax.all_to_all(sums, 'expert', 0, 0, tiled=True)  8.1 us
    pallas_call x2, Pallas kernels, fetch_more(): pl.pallas_call(functools.partial(fetch, at), out_shape=(VMEM((width, more...  7.51 us
    ppermute x3, starting transfers between devices, per_device(): parcels[shift] = lax.ppermute(parcels[shift], 'expert', ring)  7.01 us
    pallas_call x1, Pallas kernels, per_device(): pl.pallas_call(attend, out_shape=(jax.ShapeDtypeStruct((ROWS, width), F32...  5.49 us
    pallas_call x1, Pallas kernels, per_device(): pl.pallas_call(project, out_shape=jax.ShapeDtypeStruct((devices, ROWS, wi...  3.99 us
    all_to_all x1, starting transfers between devices, per_device(): sums_came = lax.all_to_all(sums, 'expert', 0, 0, tiled=True)  3.53 us
  transfers between devices with their start and end apart: 9, of which 5 were waited for; matrix products, arithmetic and copies ran while one was open for 0% of the time, Pallas kernels for 12%

profile of v4, /device:TPU:0, one launch (start us, length us, event | category | flops | bytes accessed | tf_op | source)
XLA Modules:
  0.0 87.8 jit_solution(15979498283434052436)
XLA Ops:
  1.9 5.5 %shard_map.158 = (f32[8,6144]{1,0:T(8,128)S(1)}, bf16[4,7040]{1,0:T(4,128)(2,1)S(1)}, bf16[4,7040]{1,0:T(4,128)(2,1)S(1)}, bf16[4,7040]{1,0:T(4,128)(2,1)S(1)}, ...) custom-call(s32[1]{0:T(128)S(6)} %copy.17.lengths, ...), custom_call_target="tpu_custom_call" | custom-call | tf_op jit(solution)/shard_map/pallas_call | solution.py:580
  7.4 3.1 %collective-permute-start = (bf16[4,7040]{1,0:T(4,128)(2,1)S(1)}, bf16[4,7040]{1,0:T(4,128)(2,1)S(1)}, u32[]{:S(2)}, u32[]{:S(2)}) collective-permute-start(bf16[4,7040]{1,0:T(4,128)(2,1)S(1)} %get-tuple-element.33), channel_id=1, source_target_pairs={{0,4},{1,5},{2,6},{3,7},{4,8},{5,9},{6,10},{7,11},{8,12},{9,13},{1... | collective-permute-start | bytes 168968 | tf_op jit(solution)/shard_map/ppermute | solution.py:642
  10.5 2.6 %collective-permute-start.1 = (bf16[4,7040]{1,0:T(4,128)(2,1)S(1)}, bf16[4,7040]{1,0:T(4,128)(2,1)S(1)}, u32[]{:S(2)}, u32[]{:S(2)}) collective-permute-start(bf16[4,7040]{1,0:T(4,128)(2,1)S(1)} %get-tuple-element.34), channel_id=1, source_target_pairs={{0,8},{1,9},{2,10},{3,11},{4,12},{5,13},{6,14},{7,15},{8,0},{9,1},... | collective-permute-start | bytes 168968 | tf_op jit(solution)/shard_map/ppermute | solution.py:642
  13.1 1.3 %collective-permute-start.2 = (bf16[4,7040]{1,0:T(4,128)(2,1)S(1)}, bf16[4,7040]{1,0:T(4,128)(2,1)S(1)}, u32[]{:S(2)}, u32[]{:S(2)}) collective-permute-start(bf16[4,7040]{1,0:T(4,128)(2,1)S(1)} %get-tuple-element.35), channel_id=1, source_target_pairs={{0,12},{1,13},{2,14},{3,15},{4,0},{5,1},{6,2},{7,3},{8,4},{9,5},{1... | collective-permute-start | bytes 168968 | tf_op jit(solution)/shard_map/ppermute | solution.py:642
  14.4 2.9 %shard_map.159 = (bf16[6144,256]{1,0:T(8,128)(2,1)S(1)}, bf16[6144,256]{1,0:T(8,128)(2,1)S(1)}) custom-call(f32[8,32]{1,0:T(8,128)S(1)} %get-tuple-element.30.after.placing, bf16[6144,2048]{1,0:T(8,128)(2,1)} %refs_10_.1, bf16[6144,2048]{1,0:T(8,128)(2,1)} %refs_11_.1), custom_call_target="tpu_custom_call" | custom-call | bytes 12582912 | tf_op jit(solution)/shard_map/pallas_call | solution.py:628
  17.3 0.0 collective-permute-done.refs_1_
  17.3 0.0 collective-permute-done.1.refs_2_
  17.3 0.1 collective-permute-done.2.refs_3_
  17.5 1.6 %collective-permute-start.3 = (bf16[4,4,7040]{2,1,0:T(4,128)(2,1)S(1)}, bf16[4,4,7040]{2,1,0:T(4,128)(2,1)S(1)}, u32[]{:S(2)}, u32[]{:S(2)}) collective-permute-start(bf16[4,4,7040]{2,1,0:T(4,128)(2,1)S(1)} %shard_map.160.after.refs_0_), channel_id=1, source_target_pairs={{0,2},{1,3},{2,0},{3,1},{4,6},{5,7},{6,4},{7,5},{8,10},{9,11},{10,... | collective-permute-start | bytes 675848 | tf_op jit(solution)/shard_map/ppermute | solution.py:575
  19.1 0.0 collective-permute-start.4
  19.1 4.6 %shard_map.161 = (bf16[6144,512]{1,0:T(8,128)(2,1)S(1)}, bf16[6144,512]{1,0:T(8,128)(2,1)S(1)}) custom-call(bf16[4,4,7040]{2,1,0:T(4,128)(2,1)S(1)} %shard_map.160.after.refs_0_, bf16[6144,2048]{1,0:T(8,128)(2,1)} %refs_10_.1, bf16[6144,2048]{1,0:T(8,128)(2,1)} %refs_11_.1), custom_call_target="tpu_custom_call" | custom-call | bytes 25165824 | tf_op jit(solution)/shard_map/pallas_call | solution.py:628
  23.8 0.2 collective-permute-done.3.refs_1_
  23.9 0.4 collective-permute-start.5
  24.3 0.0 collective-permute-done.4.refs_2_
  24.3 1.1 %collective-permute-done.5.refs_3_ = bf16[4,4,7040]{2,1,0:T(4,128)(2,1)S(1)} collective-permute-done((bf16[4,4,7040]{2,1,0:T(4,128)(2,1)S(1)}, bf16[4,4,7040]{2,1,0:T(4,128)(2,1)S(1)}, u32[]{:S(2)}, u32[]{:S(2)}) %collective-permute-start.5) | collective-permute-done | bytes 225312 | tf_op jit(solution)/shard_map/ppermute | solution.py:575
  25.5 18.9 %shard_map.162 = (f32[32,6144]{1,0:T(8,128)S(1)}, bf16[32,6144]{1,0:T(8,128)(2,1)S(1)}, bf16[64,768]{1,0:T(8,128)(2,1)S(1)}, f32[64,128]{1,0:T(8,128)S(1)}) custom-call(bf16[4,4,7040]{2,1,0:T(4,128)(2,1)S(1)} %shard_map.160.after.refs_0_, bf16[4,4,7040]{2,1,0:T(4,128)(2,1)S(1)} %collective-permute-done.3.refs_1_, ...), custom_call_target="tpu_custom_call" | custom-call | flops 4831838208 | bytes 75497472 | tf_op jit(solution)/shard_map/pallas_call | solution.py:665
  44.4 0.4 collective-permute-start.6
  44.8 2.4 %shard_map.163 = (bf16[768,3072]{1,0:T(8,128)(2,1)S(1)}, f32[16,768]{1,0:T(8,128)S(1)}) custom-call(bf16[64,768]{1,0:T(8,128)(2,1)S(1)} %get-tuple-element.49.notes, bf16[768,6144]{1,0:T(8,128)(2,1)} %fc.3), custom_call_target="tpu_custom_call" | custom-call | bytes 9437184 | tf_op jit(solution)/shard_map/pallas_call | solution.py:696
  47.2 0.0 collective-permute-done.6.came
  47.2 0.8 shard_map.164
  48.0 21.3 %all_to_all.10.came = bf16[8,4,9216]{2,1,0:T(4,128)(2,1)S(1)} all-to-all(bf16[8,4,9216]{2,1,0:T(4,128)(2,1)S(1)} %get-tuple-element.53), channel_id=1, replica_groups={{0,2,4,6,8,10,12,14},{1,3,5,7,9,11,13,15},{16,18,20,22,24,26,28,30},{17..., dimensions={0} | all-to-all | bytes 1179648 | tf_op jit(solution)/shard_map/all_to_all | solution.py:728
  69.3 0.1 collective-permute-start.7
  69.4 1.2 %collective-permute-done.7.other = f32[8,1536]{1,0:T(8,128)S(1)} collective-permute-done((f32[8,1536]{1,0:T(8,128)S(1)}, f32[8,1536]{1,0:T(8,128)S(1)}, u32[]{:S(2)}, u32[]{:S(2)}) %collective-permute-start.7) | collective-permute-done | bytes 49184 | tf_op jit(solution)/shard_map/ppermute | solution.py:575
  70.6 4.0 %shard_map.167 = bf16[16,8,768]{2,1,0:T(8,128)(2,1)} custom-call(f32[8,1536]{1,0:T(8,128)S(1)} %shard_map.166.mine, f32[8,1536]{1,0:T(8,128)S(1)} %collective-permute-done.7.other, f32[16,768]{1,0:T(8,128)S(1)} %get-tuple-element.54.early, bf16[768,3072]{1,0:T(8,128)(2,1)S(1)} %get-tuple-element.55.fc_first, bf16[768,6144]{1,0:T(8,128)(2,1)} %fc.3), custom_call_target="tpu_custom_call" | custom-call | tf_op jit(solution)/shard_map/pallas_call | solution.py:744
  74.6 3.5 %all-to-all-start.1 = ((bf16[16,8,768]{2,1,0:T(8,128)(2,1)}), bf16[16,8,768]{2,1,0:T(8,128)(2,1)S(1)}, u32[]{:S(2)}, u32[]{:S(2)}) async-start(bf16[16,8,768]{2,1,0:T(8,128)(2,1)} %shard_map.167), calls=%async_computation.1 | async-start | bytes 393216 | tf_op jit(solution)/shard_map/all_to_all | solution.py:756
  78.2 0.9 shard_map.165
  79.0 8.1 %all-to-all-done.1.came = bf16[16,8,768]{2,1,0:T(8,128)(2,1)S(1)} async-done(((bf16[16,8,768]{2,1,0:T(8,128)(2,1)}), bf16[16,8,768]{2,1,0:T(8,128)(2,1)S(1)}, u32[]{:S(2)}, u32[]{:S(2)}) %all-to-all-start.1) | async-done | bytes 196640 | tf_op jit(solution)/shard_map/all_to_all | solution.py:756
  87.1 0.6 shard_map.168
  (2 shorter events, 0.0 us)
Async XLA Ops:
  7.4 9.9 %collective-permute-start = (bf16[4,7040]{1,0:T(4,128)(2,1)S(1)}, bf16[4,7040]{1,0:T(4,128)(2,1)S(1)}, u32[]{:S(2)}, u32[]{:S(2)}) collective-permute-start(bf16[4,7040]{1,0:T(4,128)(2,1)S(1)} %get-tuple-element.33), channel_id=1, source_target_pairs={{0,4},{1,5},{2,6},{3,7},{4,8},{5,9},{6,10},{7,11},{8,12},{9,13},{1... | collective-permute-start | bytes 168968 | tf_op jit(solution)/shard_map/ppermute | solution.py:642
  10.5 6.8 %collective-permute-start.1 = (bf16[4,7040]{1,0:T(4,128)(2,1)S(1)}, bf16[4,7040]{1,0:T(4,128)(2,1)S(1)}, u32[]{:S(2)}, u32[]{:S(2)}) collective-permute-start(bf16[4,7040]{1,0:T(4,128)(2,1)S(1)} %get-tuple-element.34), channel_id=1, source_target_pairs={{0,8},{1,9},{2,10},{3,11},{4,12},{5,13},{6,14},{7,15},{8,0},{9,1},... | collective-permute-start | bytes 168968 | tf_op jit(solution)/shard_map/ppermute | solution.py:642
  13.1 4.4 %collective-permute-start.2 = (bf16[4,7040]{1,0:T(4,128)(2,1)S(1)}, bf16[4,7040]{1,0:T(4,128)(2,1)S(1)}, u32[]{:S(2)}, u32[]{:S(2)}) collective-permute-start(bf16[4,7040]{1,0:T(4,128)(2,1)S(1)} %get-tuple-element.35), channel_id=1, source_target_pairs={{0,12},{1,13},{2,14},{3,15},{4,0},{5,1},{6,2},{7,3},{8,4},{9,5},{1... | collective-permute-start | bytes 168968 | tf_op jit(solution)/shard_map/ppermute | solution.py:642
  17.5 6.5 %collective-permute-start.3 = (bf16[4,4,7040]{2,1,0:T(4,128)(2,1)S(1)}, bf16[4,4,7040]{2,1,0:T(4,128)(2,1)S(1)}, u32[]{:S(2)}, u32[]{:S(2)}) collective-permute-start(bf16[4,4,7040]{2,1,0:T(4,128)(2,1)S(1)} %shard_map.160.after.refs_0_), channel_id=1, source_target_pairs={{0,2},{1,3},{2,0},{3,1},{4,6},{5,7},{6,4},{7,5},{8,10},{9,11},{10,... | collective-permute-start | bytes 675848 | tf_op jit(solution)/shard_map/ppermute | solution.py:575
  19.1 5.2 %collective-permute-start.4 = (bf16[4,4,7040]{2,1,0:T(4,128)(2,1)S(1)}, bf16[4,4,7040]{2,1,0:T(4,128)(2,1)S(1)}, u32[]{:S(2)}, u32[]{:S(2)}) collective-permute-start(bf16[4,4,7040]{2,1,0:T(4,128)(2,1)S(1)} %shard_map.160.after.refs_0_), channel_id=1, source_target_pairs={{0,1},{1,0},{2,3},{3,2},{4,5},{5,4},{6,7},{7,6},{8,9},{9,8},{10,11... | collective-permute-start | bytes 675848 | tf_op jit(solution)/shard_map/ppermute | solution.py:575
  23.9 1.5 %collective-permute-start.5 = (bf16[4,4,7040]{2,1,0:T(4,128)(2,1)S(1)}, bf16[4,4,7040]{2,1,0:T(4,128)(2,1)S(1)}, u32[]{:S(2)}, u32[]{:S(2)}) collective-permute-start(bf16[4,4,7040]{2,1,0:T(4,128)(2,1)S(1)} %collective-permute-done.3.refs_1_), channel_id=1, source_target_pairs={{0,1},{1,0},{2,3},{3,2},{4,5},{5,4},{6,7},{7,6},{8,9},{9,8},{10,11... | collective-permute-start | bytes 675848 | tf_op jit(solution)/shard_map/ppermute | solution.py:575
  44.4 2.8 %collective-permute-start.6 = (bf16[32,6144]{1,0:T(8,128)(2,1)S(1)}, bf16[32,6144]{1,0:T(8,128)(2,1)S(1)}, u32[]{:S(2)}, u32[]{:S(2)}) collective-permute-start(bf16[32,6144]{1,0:T(8,128)(2,1)S(1)} %get-tuple-element.48), channel_id=1, source_target_pairs={{0,1},{1,0},{2,3},{3,2},{4,5},{5,4},{6,7},{7,6},{8,9},{9,8},{10,11... | collective-permute-start | bytes 1179656 | tf_op jit(solution)/shard_map/ppermute | solution.py:575
  69.3 1.3 %collective-permute-start.7 = (f32[8,1536]{1,0:T(8,128)S(1)}, f32[8,1536]{1,0:T(8,128)S(1)}, u32[]{:S(2)}, u32[]{:S(2)}) collective-permute-start(f32[8,1536]{1,0:T(8,128)S(1)} %shard_map.166.mine), channel_id=1, source_target_pairs={{0,1},{1,0},{2,3},{3,2},{4,5},{5,4},{6,7},{7,6},{8,9},{9,8},{10,11... | collective-permute-start | bytes 147464 | tf_op jit(solution)/shard_map/ppermute | solution.py:575
  74.6 12.5 %all-to-all-start.1 = ((bf16[16,8,768]{2,1,0:T(8,128)(2,1)}), bf16[16,8,768]{2,1,0:T(8,128)(2,1)S(1)}, u32[]{:S(2)}, u32[]{:S(2)}) async-start(bf16[16,8,768]{2,1,0:T(8,128)(2,1)} %shard_map.167), calls=%async_computation.1 | async-start | bytes 393216 | tf_op jit(solution)/shard_map/all_to_all | solution.py:756

commit v5 on v4

--- a/solution.py
+++ b/solution.py
@@ -692,7 +692,7 @@
         far(down_weight),
     )
     came = swap(send, 1)
-    fc_ready = width // 2
+    fc_ready = width // 4
     fc_first, early = pl.pallas_call(
         functools.partial(draft_fetch, masks),
         out_shape=(

time: 88.1 us -> 87.8 us (level)
  no operation moved by 1% of the time
where the time goes in v5:
time: 87.8 us; the launch traced here: 87.4 us
  Pallas kernels  40.3 us (46%)
  blocking collectives  21.3 us (24%)
  starting transfers between devices  13.1 us (15%)
  waiting for transfers between devices  10.7 us (12%)
  between operations  2.03 us (2%)
    all_to_all x1, blocking collectives, per_device(): lax.all_to_all(partial, 'expert', 0, 0, tiled=True, axis_index_groups=sam...  21.3 us
    pallas_call x1, Pallas kernels, per_device(): pl.pallas_call(functools.partial(experts, width, len(pieces), len(ready)...  18.9 us
    all_to_all x1, waiting for transfers between devices, per_device(): sums_came = lax.all_to_all(sums, 'expert', 0, 0, tiled=True)  8.1 us
    pallas_call x2, Pallas kernels, fetch_more(): pl.pallas_call(functools.partial(fetch, at), out_shape=(VMEM((width, more...  7.51 us
    ppermute x3, starting transfers between devices, per_device(): parcels[shift] = lax.ppermute(parcels[shift], 'expert', ring)  7.01 us
    pallas_call x1, Pallas kernels, per_device(): pl.pallas_call(attend, out_shape=(jax.ShapeDtypeStruct((ROWS, width), F32...  5.49 us
    pallas_call x1, Pallas kernels, per_device(): pl.pallas_call(project, out_shape=jax.ShapeDtypeStruct((devices, ROWS, wi...  4.35 us
    all_to_all x1, starting transfers between devices, per_device(): sums_came = lax.all_to_all(sums, 'expert', 0, 0, tiled=True)  3.53 us
  transfers between devices with their start and end apart: 9, of which 5 were waited for; matrix products, arithmetic and copies ran while one was open for 0% of the time, Pallas kernels for 12%

profile of v5, /device:TPU:0, one launch (start us, length us, event | category | flops | bytes accessed | tf_op | source)
XLA Modules:
  0.0 87.4 jit_solution(8036155356100105006)
XLA Ops:
  1.9 5.5 %shard_map.158 = (f32[8,6144]{1,0:T(8,128)S(1)}, bf16[4,7040]{1,0:T(4,128)(2,1)S(1)}, bf16[4,7040]{1,0:T(4,128)(2,1)S(1)}, bf16[4,7040]{1,0:T(4,128)(2,1)S(1)}, ...) custom-call(s32[1]{0:T(128)S(6)} %copy.17.lengths, ...), custom_call_target="tpu_custom_call" | custom-call | tf_op jit(solution)/shard_map/pallas_call | solution.py:580
  7.4 3.1 %collective-permute-start = (bf16[4,7040]{1,0:T(4,128)(2,1)S(1)}, bf16[4,7040]{1,0:T(4,128)(2,1)S(1)}, u32[]{:S(2)}, u32[]{:S(2)}) collective-permute-start(bf16[4,7040]{1,0:T(4,128)(2,1)S(1)} %get-tuple-element.33), channel_id=1, source_target_pairs={{0,4},{1,5},{2,6},{3,7},{4,8},{5,9},{6,10},{7,11},{8,12},{9,13},{1... | collective-permute-start | bytes 168968 | tf_op jit(solution)/shard_map/ppermute | solution.py:642
  10.5 2.6 %collective-permute-start.1 = (bf16[4,7040]{1,0:T(4,128)(2,1)S(1)}, bf16[4,7040]{1,0:T(4,128)(2,1)S(1)}, u32[]{:S(2)}, u32[]{:S(2)}) collective-permute-start(bf16[4,7040]{1,0:T(4,128)(2,1)S(1)} %get-tuple-element.34), channel_id=1, source_target_pairs={{0,8},{1,9},{2,10},{3,11},{4,12},{5,13},{6,14},{7,15},{8,0},{9,1},... | collective-permute-start | bytes 168968 | tf_op jit(solution)/shard_map/ppermute | solution.py:642
  13.1 1.3 %collective-permute-start.2 = (bf16[4,7040]{1,0:T(4,128)(2,1)S(1)}, bf16[4,7040]{1,0:T(4,128)(2,1)S(1)}, u32[]{:S(2)}, u32[]{:S(2)}) collective-permute-start(bf16[4,7040]{1,0:T(4,128)(2,1)S(1)} %get-tuple-element.35), channel_id=1, source_target_pairs={{0,12},{1,13},{2,14},{3,15},{4,0},{5,1},{6,2},{7,3},{8,4},{9,5},{1... | collective-permute-start | bytes 168968 | tf_op jit(solution)/shard_map/ppermute | solution.py:642
  14.4 2.9 %shard_map.159 = (bf16[6144,256]{1,0:T(8,128)(2,1)S(1)}, bf16[6144,256]{1,0:T(8,128)(2,1)S(1)}) custom-call(f32[8,32]{1,0:T(8,128)S(1)} %get-tuple-element.30.after.placing, bf16[6144,2048]{1,0:T(8,128)(2,1)} %refs_10_.1, bf16[6144,2048]{1,0:T(8,128)(2,1)} %refs_11_.1), custom_call_target="tpu_custom_call" | custom-call | bytes 12582912 | tf_op jit(solution)/shard_map/pallas_call | solution.py:628
  17.3 0.0 collective-permute-done.refs_1_
  17.3 0.0 collective-permute-done.1.refs_2_
  17.3 0.1 collective-permute-done.2.refs_3_
  17.5 1.6 %collective-permute-start.3 = (bf16[4,4,7040]{2,1,0:T(4,128)(2,1)S(1)}, bf16[4,4,7040]{2,1,0:T(4,128)(2,1)S(1)}, u32[]{:S(2)}, u32[]{:S(2)}) collective-permute-start(bf16[4,4,7040]{2,1,0:T(4,128)(2,1)S(1)} %shard_map.160.after.refs_0_), channel_id=1, source_target_pairs={{0,2},{1,3},{2,0},{3,1},{4,6},{5,7},{6,4},{7,5},{8,10},{9,11},{10,... | collective-permute-start | bytes 675848 | tf_op jit(solution)/shard_map/ppermute | solution.py:575
  19.1 0.0 collective-permute-start.4
  19.1 4.6 %shard_map.161 = (bf16[6144,512]{1,0:T(8,128)(2,1)S(1)}, bf16[6144,512]{1,0:T(8,128)(2,1)S(1)}) custom-call(bf16[4,4,7040]{2,1,0:T(4,128)(2,1)S(1)} %shard_map.160.after.refs_0_, bf16[6144,2048]{1,0:T(8,128)(2,1)} %refs_10_.1, bf16[6144,2048]{1,0:T(8,128)(2,1)} %refs_11_.1), custom_call_target="tpu_custom_call" | custom-call | bytes 25165824 | tf_op jit(solution)/shard_map/pallas_call | solution.py:628
  23.8 0.2 collective-permute-done.3.refs_1_
  23.9 0.4 collective-permute-start.5
  24.3 0.0 collective-permute-done.4.refs_2_
  24.3 1.1 %collective-permute-done.5.refs_3_ = bf16[4,4,7040]{2,1,0:T(4,128)(2,1)S(1)} collective-permute-done((bf16[4,4,7040]{2,1,0:T(4,128)(2,1)S(1)}, bf16[4,4,7040]{2,1,0:T(4,128)(2,1)S(1)}, u32[]{:S(2)}, u32[]{:S(2)}) %collective-permute-start.5) | collective-permute-done | bytes 225312 | tf_op jit(solution)/shard_map/ppermute | solution.py:575
  25.5 18.9 %shard_map.162 = (f32[32,6144]{1,0:T(8,128)S(1)}, bf16[32,6144]{1,0:T(8,128)(2,1)S(1)}, bf16[64,768]{1,0:T(8,128)(2,1)S(1)}, f32[64,128]{1,0:T(8,128)S(1)}) custom-call(bf16[4,4,7040]{2,1,0:T(4,128)(2,1)S(1)} %shard_map.160.after.refs_0_, bf16[4,4,7040]{2,1,0:T(4,128)(2,1)S(1)} %collective-permute-done.3.refs_1_, ...), custom_call_target="tpu_custom_call" | custom-call | flops 4831838208 | bytes 75497472 | tf_op jit(solution)/shard_map/pallas_call | solution.py:665
  44.4 0.4 collective-permute-start.6
  44.8 1.7 %shard_map.163 = (bf16[768,1536]{1,0:T(8,128)(2,1)S(1)}, f32[16,768]{1,0:T(8,128)S(1)}) custom-call(bf16[64,768]{1,0:T(8,128)(2,1)S(1)} %get-tuple-element.49.notes, bf16[768,6144]{1,0:T(8,128)(2,1)} %fc.3), custom_call_target="tpu_custom_call" | custom-call | bytes 4718592 | tf_op jit(solution)/shard_map/pallas_call | solution.py:696
  46.5 0.0 collective-permute-done.6.came
  46.5 0.8 shard_map.164
  47.3 21.3 %all_to_all.10.came = bf16[8,4,9216]{2,1,0:T(4,128)(2,1)S(1)} all-to-all(bf16[8,4,9216]{2,1,0:T(4,128)(2,1)S(1)} %get-tuple-element.53), channel_id=1, replica_groups={{0,2,4,6,8,10,12,14},{1,3,5,7,9,11,13,15},{16,18,20,22,24,26,28,30},{17..., dimensions={0} | all-to-all | bytes 1179648 | tf_op jit(solution)/shard_map/all_to_all | solution.py:728
  68.6 0.1 collective-permute-start.7
  68.7 1.2 %collective-permute-done.7.other = f32[8,1536]{1,0:T(8,128)S(1)} collective-permute-done((f32[8,1536]{1,0:T(8,128)S(1)}, f32[8,1536]{1,0:T(8,128)S(1)}, u32[]{:S(2)}, u32[]{:S(2)}) %collective-permute-start.7) | collective-permute-done | bytes 49184 | tf_op jit(solution)/shard_map/ppermute | solution.py:575
  69.9 4.4 %shard_map.167 = bf16[16,8,768]{2,1,0:T(8,128)(2,1)} custom-call(f32[8,1536]{1,0:T(8,128)S(1)} %shard_map.166.mine, f32[8,1536]{1,0:T(8,128)S(1)} %collective-permute-done.7.other, f32[16,768]{1,0:T(8,128)S(1)} %get-tuple-element.54.early, bf16[768,1536]{1,0:T(8,128)(2,1)S(1)} %get-tuple-element.55.fc_first, bf16[768,6144]{1,0:T(8,128)(2,1)} %fc.3), custom_call_target="tpu_custom_call" | custom-call | tf_op jit(solution)/shard_map/pallas_call | solution.py:744
  74.3 3.5 %all-to-all-start.1 = ((bf16[16,8,768]{2,1,0:T(8,128)(2,1)}), bf16[16,8,768]{2,1,0:T(8,128)(2,1)S(1)}, u32[]{:S(2)}, u32[]{:S(2)}) async-start(bf16[16,8,768]{2,1,0:T(8,128)(2,1)} %shard_map.167), calls=%async_computation.1 | async-start | bytes 393216 | tf_op jit(solution)/shard_map/all_to_all | solution.py:756
  77.8 0.9 shard_map.165
  78.7 8.1 %all-to-all-done.1.came = bf16[16,8,768]{2,1,0:T(8,128)(2,1)S(1)} async-done(((bf16[16,8,768]{2,1,0:T(8,128)(2,1)}), bf16[16,8,768]{2,1,0:T(8,128)(2,1)S(1)}, u32[]{:S(2)}, u32[]{:S(2)}) %all-to-all-start.1) | async-done | bytes 196640 | tf_op jit(solution)/shard_map/all_to_all | solution.py:756
  86.8 0.6 shard_map.168
  (2 shorter events, 0.0 us)
Async XLA Ops:
  7.4 9.9 %collective-permute-start = (bf16[4,7040]{1,0:T(4,128)(2,1)S(1)}, bf16[4,7040]{1,0:T(4,128)(2,1)S(1)}, u32[]{:S(2)}, u32[]{:S(2)}) collective-permute-start(bf16[4,7040]{1,0:T(4,128)(2,1)S(1)} %get-tuple-element.33), channel_id=1, source_target_pairs={{0,4},{1,5},{2,6},{3,7},{4,8},{5,9},{6,10},{7,11},{8,12},{9,13},{1... | collective-permute-start | bytes 168968 | tf_op jit(solution)/shard_map/ppermute | solution.py:642
  10.5 6.8 %collective-permute-start.1 = (bf16[4,7040]{1,0:T(4,128)(2,1)S(1)}, bf16[4,7040]{1,0:T(4,128)(2,1)S(1)}, u32[]{:S(2)}, u32[]{:S(2)}) collective-permute-start(bf16[4,7040]{1,0:T(4,128)(2,1)S(1)} %get-tuple-element.34), channel_id=1, source_target_pairs={{0,8},{1,9},{2,10},{3,11},{4,12},{5,13},{6,14},{7,15},{8,0},{9,1},... | collective-permute-start | bytes 168968 | tf_op jit(solution)/shard_map/ppermute | solution.py:642
  13.1 4.4 %collective-permute-start.2 = (bf16[4,7040]{1,0:T(4,128)(2,1)S(1)}, bf16[4,7040]{1,0:T(4,128)(2,1)S(1)}, u32[]{:S(2)}, u32[]{:S(2)}) collective-permute-start(bf16[4,7040]{1,0:T(4,128)(2,1)S(1)} %get-tuple-element.35), channel_id=1, source_target_pairs={{0,12},{1,13},{2,14},{3,15},{4,0},{5,1},{6,2},{7,3},{8,4},{9,5},{1... | collective-permute-start | bytes 168968 | tf_op jit(solution)/shard_map/ppermute | solution.py:642
  17.5 6.5 %collective-permute-start.3 = (bf16[4,4,7040]{2,1,0:T(4,128)(2,1)S(1)}, bf16[4,4,7040]{2,1,0:T(4,128)(2,1)S(1)}, u32[]{:S(2)}, u32[]{:S(2)}) collective-permute-start(bf16[4,4,7040]{2,1,0:T(4,128)(2,1)S(1)} %shard_map.160.after.refs_0_), channel_id=1, source_target_pairs={{0,2},{1,3},{2,0},{3,1},{4,6},{5,7},{6,4},{7,5},{8,10},{9,11},{10,... | collective-permute-start | bytes 675848 | tf_op jit(solution)/shard_map/ppermute | solution.py:575
  19.1 5.2 %collective-permute-start.4 = (bf16[4,4,7040]{2,1,0:T(4,128)(2,1)S(1)}, bf16[4,4,7040]{2,1,0:T(4,128)(2,1)S(1)}, u32[]{:S(2)}, u32[]{:S(2)}) collective-permute-start(bf16[4,4,7040]{2,1,0:T(4,128)(2,1)S(1)} %shard_map.160.after.refs_0_), channel_id=1, source_target_pairs={{0,1},{1,0},{2,3},{3,2},{4,5},{5,4},{6,7},{7,6},{8,9},{9,8},{10,11... | collective-permute-start | bytes 675848 | tf_op jit(solution)/shard_map/ppermute | solution.py:575
  23.9 1.5 %collective-permute-start.5 = (bf16[4,4,7040]{2,1,0:T(4,128)(2,1)S(1)}, bf16[4,4,7040]{2,1,0:T(4,128)(2,1)S(1)}, u32[]{:S(2)}, u32[]{:S(2)}) collective-permute-start(bf16[4,4,7040]{2,1,0:T(4,128)(2,1)S(1)} %collective-permute-done.3.refs_1_), channel_id=1, source_target_pairs={{0,1},{1,0},{2,3},{3,2},{4,5},{5,4},{6,7},{7,6},{8,9},{9,8},{10,11... | collective-permute-start | bytes 675848 | tf_op jit(solution)/shard_map/ppermute | solution.py:575
  44.4 2.1 %collective-permute-start.6 = (bf16[32,6144]{1,0:T(8,128)(2,1)S(1)}, bf16[32,6144]{1,0:T(8,128)(2,1)S(1)}, u32[]{:S(2)}, u32[]{:S(2)}) collective-permute-start(bf16[32,6144]{1,0:T(8,128)(2,1)S(1)} %get-tuple-element.48), channel_id=1, source_target_pairs={{0,1},{1,0},{2,3},{3,2},{4,5},{5,4},{6,7},{7,6},{8,9},{9,8},{10,11... | collective-permute-start | bytes 1179656 | tf_op jit(solution)/shard_map/ppermute | solution.py:575
  68.6 1.3 %collective-permute-start.7 = (f32[8,1536]{1,0:T(8,128)S(1)}, f32[8,1536]{1,0:T(8,128)S(1)}, u32[]{:S(2)}, u32[]{:S(2)}) collective-permute-start(f32[8,1536]{1,0:T(8,128)S(1)} %shard_map.166.mine), channel_id=1, source_target_pairs={{0,1},{1,0},{2,3},{3,2},{4,5},{5,4},{6,7},{7,6},{8,9},{9,8},{10,11... | collective-permute-start | bytes 147464 | tf_op jit(solution)/shard_map/ppermute | solution.py:575
  74.3 12.5 %all-to-all-start.1 = ((bf16[16,8,768]{2,1,0:T(8,128)(2,1)}), bf16[16,8,768]{2,1,0:T(8,128)(2,1)S(1)}, u32[]{:S(2)}, u32[]{:S(2)}) async-start(bf16[16,8,768]{2,1,0:T(8,128)(2,1)} %shard_map.167), calls=%async_computation.1 | async-start | bytes 393216 | tf_op jit(solution)/shard_map/all_to_all | solution.py:756
